TPU v7x, 128 devices: a whole 4x4x4 slice. The times are simulated.
128 devices in a mesh: seq: 8 (over x, core), wshard: 16 (over z, y).
Axes of the slice: x: 4, y: 4, z: 4, core: 2. Of those that a mesh axis runs over, the one named last changes fastest.
Arguments:
- tokens: bfloat16 [16, 1024, 1024], P('wshard', 'seq'), may hold values from -6 to 6
- weight_qkv: bfloat16 [1024, 2048], P(('seq', 'wshard')), may hold values from -0.5 to 0.5
- weight_out: bfloat16 [1024, 1024], P(('seq', 'wshard')), may hold values from -2 to 2
- router: bfloat16 [1024, 32], P(('seq', 'wshard')), may hold values from -0.09375 to 0.09375
- gain_attn: bfloat16 [1024], P(('seq', 'wshard')), may hold values from 0.5 to 1.5
- gain_ffn: bfloat16 [1024], P(('seq', 'wshard')), may hold values from 0.5 to 1.5
- expert_gate: bfloat16 [32, 1024, 512], P('wshard', 'seq'), may hold values from -0.1875 to 0.1875
- expert_up: bfloat16 [32, 1024, 512], P('wshard', 'seq'), may hold values from -0.1875 to 0.1875
- expert_down: bfloat16 [32, 512, 1024], P('wshard', 'seq'), may hold values from -2 to 2
- expert_ids: int32 [16, 1024, 8], P('wshard', 'seq'), may hold values from 0 to 31, all different within a row; in each aligned block of 128 rows (0 to 127, 128 to 255, ..., all dimensions but the last counted through in order) at most 64 rows name the same one
- cotangent: bfloat16 [16, 1024, 1024], P('wshard', 'seq'), may hold values from -6 to 6
Outputs:
- output: bfloat16 [16, 1024, 1024], P('wshard', 'seq')
- grad_tokens: bfloat16 [16, 1024, 1024], P('wshard', 'seq')
- grad_qkv: float32 [1024, 2048], P(('seq', 'wshard'))
- grad_out: float32 [1024, 1024], P(('seq', 'wshard'))
- grad_router: float32 [1024, 32], P(('seq', 'wshard'))
- grad_gain_attn: float32 [1024], P(('seq', 'wshard'))
- grad_gain_ffn: float32 [1024], P(('seq', 'wshard'))
- grad_gate: float32 [32, 1024, 512], P('wshard', 'seq')
- grad_up: float32 [32, 1024, 512], P('wshard', 'seq')
- grad_down: float32 [32, 512, 1024], P('wshard', 'seq')
Inputs may be any that keep to these rules, and one draw needn't show every extreme that they name: `expert_ids`: each row names 8 different experts. In the 128 rows of one device (aligned blocks of each sequence) no expert is named more than 64 times, and in every draw some expert is named exactly 64 times in some block.
All inputs are finite; a program needn't handle non-finite values.
Results may differ from a plain program's by a relative error of at most 0.02.
Values may be sent and summed in bfloat16 or wider, within the bound.
A program may use at most 128 MiB of HBM per device.

v0:
```python
import jax
import jax.numpy as jnp
from jax import lax
from jax.sharding import PartitionSpec as P

HEADS = 16
KV_HEADS = 8
HEAD_DIM = 64


epsilon = 1e-06
attention_multiplier = 0.015625
residual_multiplier = 0.22
rope_theta = 10000.0


def rms_scale(values):
    return lax.rsqrt(jnp.mean(values * values, axis=-1, keepdims=True) + epsilon)


def rotate(heads_in, positions, direction):
    half_dim = heads_in.shape[-1] // 2
    frequency = rope_theta ** (-jnp.arange(half_dim, dtype=jnp.float32) / half_dim)
    angles = positions.astype(jnp.float32)[:, None] * frequency[None, :]
    cosine = jnp.cos(angles)[:, None, :]
    sine_of = direction * jnp.sin(angles)[:, None, :]
    leading = heads_in[..., :half_dim]
    second = heads_in[..., half_dim:]
    return jnp.concatenate(
        [leading * cosine - second * sine_of, second * cosine + leading * sine_of], axis=-1
    )


def attend_forward(queries, keys_all, values_all):
    length, heads_dev, head_size = queries.shape
    key_heads = keys_all.shape[1]
    group_size = heads_dev // key_heads
    block_rows = min(512, length)
    block_count = length // block_rows
    grouped = queries.reshape(block_count, block_rows, key_heads, group_size, head_size)
    starts = jnp.arange(block_count, dtype=jnp.int32) * block_rows
    key_pos = jnp.arange(length, dtype=jnp.int32)

    def one_block(operands):
        rows_in, offset = operands
        scores = attention_multiplier * jnp.einsum(
            "qhrd,khd->hrqk", rows_in, keys_all, preferred_element_type=jnp.float32
        )
        allowed = key_pos[None, :] <= (offset + jnp.arange(block_rows, dtype=jnp.int32))[:, None]
        scores = jnp.where(allowed, scores, -1e30)
        peak_score = jnp.max(scores, axis=-1, keepdims=True)
        exponent = jnp.exp(scores - peak_score)
        total = jnp.sum(exponent, axis=-1, keepdims=True)
        weights = (exponent / total).astype(jnp.bfloat16)
        blended = jnp.einsum(
            "hrqk,khd->qhrd", weights, values_all, preferred_element_type=jnp.float32
        )
        return (
            blended.reshape(block_rows, heads_dev * head_size),
            (peak_score + jnp.log(total))[..., 0],
        )

    blended, logsum = lax.map(one_block, (grouped, starts))
    return (blended.reshape(length, heads_dev * head_size), logsum)


def attend_backward(queries, keys_all, values_all, grads_out, logsum):
    length, heads_dev, head_size = queries.shape
    key_heads = keys_all.shape[1]
    group_size = heads_dev // key_heads
    block_rows = min(512, length)
    block_count = length // block_rows
    grouped = queries.reshape(block_count, block_rows, key_heads, group_size, head_size)
    grads_grouped = grads_out.reshape(block_count, block_rows, key_heads, group_size, head_size)
    starts = jnp.arange(block_count, dtype=jnp.int32) * block_rows
    key_pos = jnp.arange(length, dtype=jnp.int32)

    def one_block(carry, operands):
        rows_in, grads_in, block_lse, offset = operands
        scores = attention_multiplier * jnp.einsum(
            "qhrd,khd->hrqk", rows_in, keys_all, preferred_element_type=jnp.float32
        )
        allowed = key_pos[None, :] <= (offset + jnp.arange(block_rows, dtype=jnp.int32))[:, None]
        weights = jnp.where(allowed, jnp.exp(scores - block_lse[..., None]), 0.0)
        grad_weights = jnp.einsum(
            "qhrd,khd->hrqk", grads_in, values_all, preferred_element_type=jnp.float32
        )
        center = jnp.sum(weights * grad_weights, axis=-1, keepdims=True)
        grad_scores = (weights * (grad_weights - center)).astype(jnp.bfloat16)
        grad_rows = attention_multiplier * jnp.einsum(
            "hrqk,khd->qhrd", grad_scores, keys_all, preferred_element_type=jnp.float32
        )
        grad_keys = carry[0] + attention_multiplier * jnp.einsum(
            "hrqk,qhrd->khd", grad_scores, rows_in, preferred_element_type=jnp.float32
        )
        grad_values = carry[1] + jnp.einsum(
            "hrqk,qhrd->khd",
            weights.astype(jnp.bfloat16),
            grads_in,
            preferred_element_type=jnp.float32,
        )
        return ((grad_keys, grad_values), grad_rows.reshape(block_rows, heads_dev, head_size))

    zeros_kv = jnp.zeros((length, key_heads, head_size), jnp.float32)
    totals, grad_queries = lax.scan(
        one_block, (zeros_kv, zeros_kv), (grouped, grads_grouped, logsum, starts)
    )
    return (grad_queries.reshape(length, heads_dev, head_size), totals[0], totals[1])


def route_slots(chosen_ids, experts_all):
    flat_ids = chosen_ids.reshape(-1)
    onehot = (flat_ids[:, None] == jnp.arange(experts_all, dtype=jnp.int32)[None, :]).astype(
        jnp.int32
    )
    places = jnp.cumsum(onehot, axis=0) - 1
    return (flat_ids, jnp.sum(places * onehot, axis=1))


def dispatch_rows(buffer, owners):
    experts_all, capacity, features = buffer.shape
    shaped = buffer.reshape(owners, experts_all // owners, capacity, features)
    arrived = lax.all_to_all(shaped, "wshard", split_axis=0, concat_axis=2, tiled=True)
    return arrived.reshape(experts_all // owners, owners * capacity, features)


def combine_rows(results, owners):
    local_experts, received_rows, features = results.shape
    shaped = results.reshape(local_experts, owners, received_rows // owners, features)
    arrived = lax.all_to_all(shaped, "wshard", split_axis=1, concat_axis=0, tiled=True)
    return arrived.reshape(local_experts * owners, received_rows // owners, features)


def dispatch_grads(buffer, owners):
    experts_all, capacity, features = buffer.shape
    shaped = buffer.reshape(owners, experts_all // owners, capacity, features)
    arrived = lax.all_to_all(shaped, "wshard", split_axis=0, concat_axis=2, tiled=True)
    return arrived.reshape(experts_all // owners, owners * capacity, features)


def combine_grads(results, owners):
    local_experts, received_rows, features = results.shape
    shaped = results.reshape(local_experts, owners, received_rows // owners, features)
    arrived = lax.all_to_all(shaped, "wshard", split_axis=1, concat_axis=0, tiled=True)
    return arrived.reshape(local_experts * owners, received_rows // owners, features)


def norm_backward(grad_normed, values, scale, gain_full):
    grad_gain = jnp.sum(grad_normed * values * scale, axis=0)
    grad_hat = grad_normed * gain_full
    grad_values = scale * grad_hat - values * (scale * scale * scale) * jnp.mean(
        grad_hat * values, axis=1, keepdims=True
    )
    return (grad_values, grad_gain)


def local(
    tokens,
    weight_qkv,
    weight_out,
    router,
    gain_attn,
    gain_ffn,
    expert_gate,
    expert_up,
    expert_down,
    expert_ids,
    cotangent,
):
    tok_dev = tokens.shape[1]
    features = tokens.shape[2]
    seq_parts = lax.axis_size("seq")
    owners = lax.axis_size("wshard")
    local_experts = expert_gate.shape[0]
    experts_all = local_experts * owners
    top_count = expert_ids.shape[2]
    capacity = 2 * tok_dev * top_count // experts_all
    heads_dev = HEADS // seq_parts
    key_heads = KV_HEADS // seq_parts
    query_cols = heads_dev * HEAD_DIM
    key_cols = key_heads * HEAD_DIM
    query_width = HEADS * HEAD_DIM
    key_width = KV_HEADS * HEAD_DIM
    length = tok_dev * seq_parts
    fetched = (
        lax.all_gather(weight_qkv, ("seq", "wshard"), axis=0, tiled=True),
        lax.all_gather(weight_out, ("seq", "wshard"), axis=0, tiled=True),
        lax.all_gather(router, ("seq", "wshard"), axis=0, tiled=True),
        lax.all_gather(gain_attn, ("seq", "wshard"), axis=0, tiled=True),
        lax.all_gather(gain_ffn, ("seq", "wshard"), axis=0, tiled=True),
    )
    qkv_full, out_full, router_full = (fetched[0], fetched[1], fetched[2])
    gain_one = fetched[3].astype(jnp.float32)
    gain_two = fetched[4].astype(jnp.float32)
    owned = (
        lax.all_gather(expert_gate, "seq", axis=1, tiled=True),
        lax.all_gather(expert_up, "seq", axis=1, tiled=True),
        lax.all_gather(expert_down, "seq", axis=1, tiled=True),
    )
    gate_full, up_full, down_full = (owned[0], owned[1], owned[2])
    inputs = tokens[0].astype(jnp.float32)
    chosen_ids = expert_ids[0]
    scale_one = rms_scale(inputs)
    normed_one = (inputs * scale_one * gain_one).astype(jnp.bfloat16)
    projected = jnp.dot(normed_one, qkv_full, preferred_element_type=jnp.float32)
    positions = lax.axis_index("seq") * tok_dev + jnp.arange(tok_dev, dtype=jnp.int32)
    queries = rotate(projected[:, :query_width].reshape(tok_dev, HEADS, HEAD_DIM), positions, 1.0)
    keys_tok = rotate(
        projected[:, query_width : query_width + key_width].reshape(tok_dev, KV_HEADS, HEAD_DIM),
        positions,
        1.0,
    )
    values_tok = projected[:, query_width + key_width :]
    packed = jnp.concatenate(
        [
            queries.reshape(tok_dev, seq_parts, query_cols),
            keys_tok,
            values_tok.reshape(tok_dev, seq_parts, key_cols),
        ],
        axis=2,
    ).astype(jnp.bfloat16)
    heads_all = lax.all_to_all(packed, "seq", split_axis=1, concat_axis=0, tiled=True)
    head_queries = heads_all[:, 0, :query_cols].reshape(length, heads_dev, HEAD_DIM)
    head_keys = heads_all[:, 0, query_cols : query_cols + key_cols].reshape(
        length, key_heads, HEAD_DIM
    )
    head_values = heads_all[:, 0, query_cols + key_cols :].reshape(length, key_heads, HEAD_DIM)
    blended, logsum = attend_forward(head_queries, head_keys, head_values)
    returned_heads = lax.all_to_all(
        blended.astype(jnp.bfloat16).reshape(length, 1, query_cols),
        "seq",
        split_axis=0,
        concat_axis=1,
        tiled=True,
    )
    attended = returned_heads.reshape(tok_dev, query_width)
    branch = jnp.dot(attended, out_full, preferred_element_type=jnp.float32)
    hidden = inputs + residual_multiplier * branch
    scale_two = rms_scale(hidden)
    normed_two = (hidden * scale_two * gain_two).astype(jnp.bfloat16)
    logits = jnp.dot(normed_two, router_full, preferred_element_type=jnp.float32)
    chosen = jnp.take_along_axis(logits, chosen_ids, axis=1)
    peak_logit = jnp.max(chosen, axis=1, keepdims=True)
    exponent = jnp.exp(chosen - peak_logit)
    gate_share = exponent / jnp.sum(exponent, axis=1, keepdims=True)
    flat_ids, slot_of = route_slots(chosen_ids, experts_all)
    buffer = jnp.zeros((experts_all, capacity, features), jnp.bfloat16)
    buffer = buffer.at[flat_ids, slot_of].set(jnp.repeat(normed_two, top_count, axis=0))
    received = dispatch_rows(buffer, owners)
    gate_val = jnp.einsum("erd,edf->erf", received, gate_full, preferred_element_type=jnp.float32)
    up_val = jnp.einsum("erd,edf->erf", received, up_full, preferred_element_type=jnp.float32)
    sigma = jax.nn.sigmoid(gate_val)
    activated = gate_val * sigma
    inner_act = (activated * up_val).astype(jnp.bfloat16)
    produced = jnp.einsum(
        "erf,efd->erd", inner_act, down_full, preferred_element_type=jnp.float32
    ).astype(jnp.bfloat16)
    returned = combine_rows(produced, owners)
    routed = returned[flat_ids, slot_of].reshape(tok_dev, top_count, features)
    mixture = jnp.sum(gate_share[:, :, None] * routed, axis=1)
    output = hidden + residual_multiplier * mixture
    grad_output = cotangent[0].astype(jnp.float32)
    grad_mix = residual_multiplier * grad_output
    grad_gates = jnp.sum(routed * grad_mix[:, None, :], axis=-1)
    grad_chosen = gate_share * (
        grad_gates - jnp.sum(gate_share * grad_gates, axis=1, keepdims=True)
    )
    onehot_route = (
        chosen_ids[:, :, None] == jnp.arange(experts_all, dtype=jnp.int32)[None, None, :]
    ).astype(jnp.float32)
    grad_logits = jnp.einsum("tk,tke->te", grad_chosen, onehot_route).astype(jnp.bfloat16)
    grad_router = jnp.dot(normed_two.T, grad_logits, preferred_element_type=jnp.float32)
    grad_normed_two = jnp.dot(grad_logits, router_full.T, preferred_element_type=jnp.float32)
    grad_routed = (
        (gate_share[:, :, None] * grad_mix[:, None, :])
        .astype(jnp.bfloat16)
        .reshape(tok_dev * top_count, features)
    )
    grad_buffer = (
        jnp.zeros((experts_all, capacity, features), jnp.bfloat16)
        .at[flat_ids, slot_of]
        .set(grad_routed)
    )
    grad_received = dispatch_grads(grad_buffer, owners)
    grad_inner = jnp.einsum(
        "erd,efd->erf", grad_received, down_full, preferred_element_type=jnp.float32
    )
    grad_down = jnp.einsum(
        "erf,erd->efd", inner_act, grad_received, preferred_element_type=jnp.float32
    )
    grad_gate_val = (grad_inner * up_val * (sigma * (1.0 + gate_val * (1.0 - sigma)))).astype(
        jnp.bfloat16
    )
    grad_up_val = (grad_inner * activated).astype(jnp.bfloat16)
    grad_rows = (
        jnp.einsum("erf,edf->erd", grad_gate_val, gate_full, preferred_element_type=jnp.float32)
        + jnp.einsum("erf,edf->erd", grad_up_val, up_full, preferred_element_type=jnp.float32)
    ).astype(jnp.bfloat16)
    grad_gate = jnp.einsum(
        "erd,erf->edf", received, grad_gate_val, preferred_element_type=jnp.float32
    )
    grad_up = jnp.einsum("erd,erf->edf", received, grad_up_val, preferred_element_type=jnp.float32)
    expert_shares = (
        lax.psum_scatter(
            grad_gate.astype(jnp.bfloat16), "seq", scatter_dimension=1, tiled=True
        ).astype(jnp.float32),
        lax.psum_scatter(
            grad_up.astype(jnp.bfloat16), "seq", scatter_dimension=1, tiled=True
        ).astype(jnp.float32),
        lax.psum_scatter(
            grad_down.astype(jnp.bfloat16), "seq", scatter_dimension=1, tiled=True
        ).astype(jnp.float32),
    )
    grad_back = combine_grads(grad_rows, owners)
    grad_normed_two = grad_normed_two + jnp.sum(
        grad_back[flat_ids, slot_of].reshape(tok_dev, top_count, features).astype(jnp.float32),
        axis=1,
    )
    grad_hidden_norm, grad_gain_ffn = norm_backward(grad_normed_two, hidden, scale_two, gain_two)
    grad_hidden = grad_output + grad_hidden_norm
    grad_branch = (residual_multiplier * grad_hidden).astype(jnp.bfloat16)
    grad_out = jnp.dot(attended.T, grad_branch, preferred_element_type=jnp.float32)
    grad_attended = jnp.dot(grad_branch, out_full.T, preferred_element_type=jnp.float32).astype(
        jnp.bfloat16
    )
    grad_heads = lax.all_to_all(
        grad_attended.reshape(tok_dev, seq_parts, query_cols),
        "seq",
        split_axis=1,
        concat_axis=0,
        tiled=True,
    )
    grad_heads = grad_heads.reshape(length, heads_dev, HEAD_DIM)
    grad_queries, grad_keys, grad_values = attend_backward(
        head_queries, head_keys, head_values, grad_heads, logsum
    )
    head_pos = jnp.arange(length, dtype=jnp.int32)
    grad_queries = rotate(grad_queries, head_pos, -1.0)
    grad_keys = rotate(grad_keys, head_pos, -1.0)
    grad_packed = jnp.concatenate(
        [
            grad_queries.reshape(length, query_cols),
            grad_keys.reshape(length, key_cols),
            grad_values.reshape(length, key_cols),
        ],
        axis=1,
    ).astype(jnp.bfloat16)
    grad_parts = lax.all_to_all(
        grad_packed.reshape(length, 1, query_cols + 2 * key_cols),
        "seq",
        split_axis=0,
        concat_axis=1,
        tiled=True,
    )
    grad_proj = jnp.concatenate(
        [
            grad_parts[:, :, :query_cols].reshape(tok_dev, query_width),
            grad_parts[:, :, query_cols : query_cols + key_cols].reshape(tok_dev, key_width),
            grad_parts[:, :, query_cols + key_cols :].reshape(tok_dev, key_width),
        ],
        axis=1,
    )
    grad_qkv = jnp.dot(normed_one.T, grad_proj, preferred_element_type=jnp.float32)
    grad_normed_one = jnp.dot(grad_proj, qkv_full.T, preferred_element_type=jnp.float32)
    grad_input_norm, grad_gain_attn = norm_backward(grad_normed_one, inputs, scale_one, gain_one)
    grad_input = grad_hidden + grad_input_norm
    shares = (
        lax.psum_scatter(grad_qkv, ("seq", "wshard"), scatter_dimension=0, tiled=True),
        lax.psum_scatter(grad_out, ("seq", "wshard"), scatter_dimension=0, tiled=True),
        lax.psum_scatter(grad_router, ("seq", "wshard"), scatter_dimension=0, tiled=True),
        lax.psum_scatter(grad_gain_attn, ("seq", "wshard"), scatter_dimension=0, tiled=True),
        lax.psum_scatter(grad_gain_ffn, ("seq", "wshard"), scatter_dimension=0, tiled=True),
    )
    return (
        output.astype(jnp.bfloat16)[None],
        grad_input.astype(jnp.bfloat16)[None],
        shares[0],
        shares[1],
        shares[2],
        shares[3],
        shares[4],
        expert_shares[0],
        expert_shares[1],
        expert_shares[2],
    )


def solution(mesh):
    placed = (
        P("wshard", "seq", None),
        P(("seq", "wshard"), None),
        P(("seq", "wshard"), None),
        P(("seq", "wshard"), None),
        P(("seq", "wshard")),
        P(("seq", "wshard")),
        P("wshard", "seq", None),
        P("wshard", "seq", None),
        P("wshard", "seq", None),
        P("wshard", "seq", None),
        P("wshard", "seq", None),
    )
    return jax.shard_map(
        local,
        mesh=mesh,
        in_specs=placed,
        out_specs=(
            P("wshard", "seq", None),
            P("wshard", "seq", None),
            P(("seq", "wshard"), None),
            P(("seq", "wshard"), None),
            P(("seq", "wshard"), None),
            P(("seq", "wshard")),
            P(("seq", "wshard")),
            P("wshard", "seq", None),
            P("wshard", "seq", None),
            P("wshard", "seq", None),
        ),
        check_vma=False,
    )
```

profile of v0, /device:TPU:0, one launch (start us, length us, event | category | flops | bytes accessed | tf_op | source)
XLA Modules:
  0.0 2055.0 jit_solution(9737166808383057686)
XLA Ops:
  12.2 69.1 %all-reduce.6 = (bf16[1024]{0:T(1024)(128)(2,1)S(1)}, bf16[1024]{0:T(1024)(128)(2,1)S(1)}) all-reduce(bf16[1024]{0:T(1024)(128)(2,1)S(1)} %dynamic-update-slice, bf16[1024]{0:T(1024)(128)(2,1)S(1)} %dynamic-update-slice.1), channel_id=1, replica_groups=mesh['seq'=8,'wshard'=16] {'seq','wshard'}, use_global_device_ids=true, to_apply=%add | all-reduce | flops 2048 | bytes 8192
  83.0 9.0 reduce-window.6
  94.2 3.1 fusion.101
  98.9 3.5 all-to-all-start
  102.5 10.2 all-to-all-done
  114.0 11.0 while.28
  127.1 3.4 all-to-all-start.1
  130.6 56.3 %all_gather.28 = bf16[1024,32]{1,0:T(8,128)(2,1)S(1)} all-gather(bf16[8,32]{1,0:T(8,128)(2,1)S(1)} %copy-done.33), channel_id=1, replica_groups=mesh['seq'=8,'wshard'=16] {'seq','wshard'}, dimensions={0}, use_global_device_ids=true | all-gather | bytes 66048 | tf_op jit(solution)/shard_map/all_gather | solution.py:188
  190.3 7.0 gather_fusion.2
  198.2 8.3 scatter_custom_fusion.1
  206.5 4.5 all-to-all-start.4
  211.6 7.9 scatter_custom_fusion
  219.5 56.9 %all-to-all-done.4 = bf16[16,2,64,1024]{3,2,1,0:T(8,128)(2,1)} async-done(((bf16[16,2,64,1024]{3,2,1,0:T(8,128)(2,1)}), bf16[16,2,64,1024]{3,2,1,0:T(8,128)(2,1)}, u32[]{:S(2)}, u32[]{:S(2)}) %all-to-all-start.4) | async-done | bytes 4194336 | tf_op jit(solution)/shard_map/all_to_all | solution.py:137
  276.4 4.5 all-to-all-start.2
  281.5 4.9 copy.144
  286.4 57.8 %all-to-all-done.2 = bf16[16,2,64,1024]{3,2,1,0:T(8,128)(2,1)} async-done(((bf16[16,2,64,1024]{3,2,1,0:T(8,128)(2,1)}), bf16[16,2,64,1024]{3,2,1,0:T(8,128)(2,1)}, u32[]{:S(2)}, u32[]{:S(2)}) %all-to-all-start.2) | async-done | bytes 4194336 | tf_op jit(solution)/shard_map/all_to_all | solution.py:123
  344.2 4.9 copy.142
  349.1 7.1 fusion.119
  356.2 7.1 fusion.120
  363.4 11.4 multiply_convert_fusion
  379.5 4.9 all-to-all-start.3
  385.4 59.4 %all-to-all-done.3 = bf16[2,16,64,1024]{3,2,0,1:T(8,128)(2,1)} async-done(((bf16[2,16,64,1024]{3,2,0,1:T(8,128)(2,1)}), bf16[2,16,64,1024]{3,2,0,1:T(8,128)(2,1)}, u32[]{:S(2)}, u32[]{:S(2)}) %all-to-all-start.3) | async-done | bytes 4194336 | tf_op jit(solution)/shard_map/all_to_all | solution.py:130
  444.8 15.3 gather_fusion
  460.1 3.6 fusion.57
  467.1 6.5 convolution_convert_fusion.1
  473.7 6.7 convolution_convert_fusion.3
  480.4 4.1 fusion.121
  489.4 4.9 all-to-all-start.5
  494.4 5.9 convolution_convert_fusion.2
  500.4 51.5 %all-to-all-done.5 = bf16[2,16,64,1024]{3,2,0,1:T(8,128)(2,1)} async-done(((bf16[2,16,64,1024]{3,2,0,1:T(8,128)(2,1)}), bf16[2,16,64,1024]{3,2,0,1:T(8,128)(2,1)}, u32[]{:S(2)}, u32[]{:S(2)}) %all-to-all-start.5) | async-done | bytes 4194336 | tf_op jit(solution)/shard_map/all_to_all | solution.py:144
  551.9 15.3 gather_fusion.1
  571.6 2.6 fusion.99
  577.7 9.3 all-to-all-start.6
  588.5 6.0 all-to-all-done.6
  594.9 34.1 %while.29 = (s32[]{:T(128)}, f32[1024,1,64]{0,2,1:T(8,128)S(1)}, f32[1024,1,64]{0,2,1:T(8,128)}, f32[2,512,2,64]{1,0,3,2:T(2,128)}, bf16[2,512,1,2,64]{1,4,3,2,0...) while((s32[]{:T(128)}, f32[1024,1,64]{0,2,1:T(8,128)S(1)}, ...), condition=%wide.region_20.21_spmd.clone, body=%wide.region_18.20_spmd.clone.sunk | while | flops 687734272 | bytes 56787876 | solution.py:105
  601.4 5.8 dynamic_update_slice.22
  607.7 4.3 fusion.189
  618.4 5.8 dynamic_update_slice.22
  624.7 4.3 fusion.189
  635.2 13.2 all_to_all.126
  649.7 4.6 fusion.84
  655.7 28.7 %reduce-scatter.14.cloned.1.call-done = bf16[2,64,1024]{2,1,0:T(8,128)(2,1)} async-done(((bf16[2,512,1024]{2,1,0:T(8,128)(2,1)}), bf16[2,64,1024]{2,1,0:T(8,128)(2,1)}) %reduce-scatter.14.cloned.1.call-update) | async-done | bytes 262160 | tf_op jit(solution)/shard_map/reduce_scatter | solution.py:310
  686.2 33.3 %reduce-scatter.10.cloned.1.call-done = bf16[2,128,512]{2,1,0:T(8,128)(2,1)} async-done(((bf16[2,1024,512]{2,1,0:T(8,128)(2,1)}), bf16[2,128,512]{2,1,0:T(8,128)(2,1)}) %reduce-scatter.10.cloned.1.call-update) | async-done | bytes 262160 | tf_op jit(solution)/shard_map/reduce_scatter | solution.py:304
  721.3 33.2 %reduce-scatter.12.cloned.1.call-done = bf16[2,128,512]{2,1,0:T(8,128)(2,1)} async-done(((bf16[2,1024,512]{2,1,0:T(8,128)(2,1)}), bf16[2,128,512]{2,1,0:T(8,128)(2,1)}) %reduce-scatter.12.cloned.1.call-update) | async-done | bytes 262160 | tf_op jit(solution)/shard_map/reduce_scatter | solution.py:307
  756.3 3.8 fusion.79
  760.1 66.3 %all-reduce.5 = (f32[1024]{0:T(1024)S(1)}, f32[1024]{0:T(1024)S(1)}) all-reduce(f32[1024]{0:T(1024)S(1)} %get-tuple-element.240, f32[1024]{0:T(1024)S(1)} %copy-done.27), channel_id=5, replica_groups=mesh['seq'=8,'wshard'=16] {'seq','wshard'}, use_global_device_ids=true, to_apply=%region_26.27.clone | all-reduce | flops 2048 | bytes 16384
  828.5 570.8 %reduce-scatter.8.cloned.1.call-done = f32[8,1024]{1,0:T(8,128)} async-done(((f32[1024,1024]{1,0:T(8,128)}), f32[8,1024]{1,0:T(8,128)}) %reduce-scatter.8.cloned.1.call-update) | async-done | bytes 32784 | tf_op jit(solution)/shard_map/reduce_scatter | solution.py:369
  1399.3 648.7 %reduce-scatter.6.cloned.1.call-done = f32[8,2048]{1,0:T(8,128)} async-done(((f32[1024,2048]{1,0:T(8,128)}), f32[8,2048]{1,0:T(8,128)}) %reduce-scatter.6.cloned.1.call-update) | async-done | bytes 65552 | tf_op jit(solution)/shard_map/reduce_scatter | solution.py:368
  (275 shorter events, 83.3 us)
Async XLA Ops:
  7.2 87.1 %all-gather.6.cloned.1.call-start = ((), (), s32[]{:S(2)}) async-start(), calls=%async_computation.13 | async-start | bytes 4227072 | tf_op jit(solution)/shard_map/all_gather | solution.py:186
  7.9 179.8 %all-gather.8.cloned.1.call-start = ((), (), s32[]{:S(2)}) async-start(), calls=%async_computation.14 | async-start | bytes 2113536 | tf_op jit(solution)/shard_map/all_gather | solution.py:187
  8.7 340.4 %all-gather.10.cloned.1.call-start = ((), (), s32[]{:S(2)}) async-start(), calls=%async_computation.15 | async-start | bytes 2359296 | tf_op jit(solution)/shard_map/all_gather | solution.py:196
  9.4 88.0 %copy-start.31 = (f32[32]{0:T(128)}, f32[32]{0:T(128)S(1)}, u32[]{:S(2)}) copy-start(f32[32]{0:T(128)S(1)} %multiply_power_fusion) | copy-start | bytes 388
  81.4 16.0 copy-start.25
  83.0 14.4 copy-start.29
  97.3 5.1 copy-start.28
  97.3 5.1 copy-start.21
  98.9 13.8 all-to-all-start
  102.5 95.6 %copy-start.9 = (f32[128,1024]{1,0:T(8,128)}, f32[128,1024]{1,0:T(8,128)S(1)}, u32[]{:S(2)}) copy-start(f32[128,1024]{1,0:T(8,128)S(1)} %convert_multiply_fusion.7) | copy-start | bytes 1572868
  114.0 16.6 copy-start.33
  125.0 62.7 %copy-start.5 = (bf16[1,128,1024]{2,1,0:T(8,128)(2,1)S(1)}, bf16[1,128,1024]{2,1,0:T(8,128)(2,1)}, u32[]{:S(2)}) copy-start(bf16[1,128,1024]{2,1,0:T(8,128)(2,1)} %param.15) | copy-start | bytes 786436
  127.1 60.0 %all-to-all-start.1 = ((bf16[8,2,8192]{2,1,0:T(2,128)(2,1)}), bf16[8,2,8192]{2,1,0:T(2,128)(2,1)S(1)}, u32[]{:S(2)}, u32[]{:S(2)}) async-start(bf16[8,2,8192]{2,1,0:T(2,128)(2,1)} %reshape.732), calls=%async_computation.1 | async-start | bytes 524288 | tf_op jit(solution)/shard_map/all_to_all | solution.py:229
  186.9 10.4 copy-start.12
  187.7 9.7 copy-start.14
  189.9 378.8 %copy-start.4 = (f32[128,1024]{1,0:T(8,128)}, f32[128,1024]{1,0:T(8,128)S(1)}, u32[]{:S(2)}) copy-start(f32[128,1024]{1,0:T(8,128)S(1)} %get-tuple-element.313) | copy-start | bytes 1572868
  206.5 69.9 %all-to-all-start.4 = ((bf16[16,2,64,1024]{3,2,1,0:T(8,128)(2,1)}), bf16[16,2,64,1024]{3,2,1,0:T(8,128)(2,1)}, u32[]{:S(2)}, u32[]{:S(2)}) async-start(bf16[16,2,64,1024]{3,2,1,0:T(8,128)(2,1)} %bitcast.368), calls=%async_computation.4 | async-start | bytes 8388608 | tf_op jit(solution)/shard_map/all_to_all | solution.py:137
  211.0 145.2 %all-gather.12.cloned.1.call-start = ((), (), s32[]{:S(2)}) async-start(), calls=%async_computation.16 | async-start | bytes 2359296 | tf_op jit(solution)/shard_map/all_gather | solution.py:197
  276.4 67.8 %all-to-all-start.2 = ((bf16[16,2,64,1024]{3,2,1,0:T(8,128)(2,1)}), bf16[16,2,64,1024]{3,2,1,0:T(8,128)(2,1)}, u32[]{:S(2)}, u32[]{:S(2)}) async-start(bf16[16,2,64,1024]{3,2,1,0:T(8,128)(2,1)} %bitcast.367), calls=%async_computation.2 | async-start | bytes 8388608 | tf_op jit(solution)/shard_map/all_to_all | solution.py:123
  281.0 82.4 %all-gather.14.cloned.1.call-start = ((), (), s32[]{:S(2)}) async-start(), calls=%async_computation.17 | async-start | bytes 2359296 | tf_op jit(solution)/shard_map/all_gather | solution.py:198
  363.4 11.4 copy-start.35
  379.5 65.3 %all-to-all-start.3 = ((bf16[2,16,64,1024]{3,2,0,1:T(8,128)(2,1)}), bf16[2,16,64,1024]{3,2,0,1:T(8,128)(2,1)}, u32[]{:S(2)}, u32[]{:S(2)}) async-start(bf16[2,16,64,1024]{3,2,0,1:T(8,128)(2,1)} %copy.143), calls=%async_computation.3 | async-start | bytes 8388608 | tf_op jit(solution)/shard_map/all_to_all | solution.py:130
  384.4 270.0 %all-reduce.9.cloned.1.call-start = ((), (), s32[]{:S(2)}) async-start(), calls=%async_computation.23 | async-start | bytes 1048576
  465.9 7.7 copy-start.23
  467.0 217.4 %reduce-scatter.14.cloned.1.call-start = ((), (), s32[]{:S(2)}) async-start(), calls=%async_computation.22 | async-start | bytes 2359296 | tf_op jit(solution)/shard_map/reduce_scatter | solution.py:310
  473.6 245.9 %reduce-scatter.10.cloned.1.call-start = ((), (), s32[]{:S(2)}) async-start(), calls=%async_computation.20 | async-start | bytes 2359296 | tf_op jit(solution)/shard_map/reduce_scatter | solution.py:304
  473.7 6.8 copy-start.17
  489.4 4.9 copy-start.20
  489.4 62.5 %all-to-all-start.5 = ((bf16[2,16,64,1024]{3,2,0,1:T(8,128)(2,1)}), bf16[2,16,64,1024]{3,2,0,1:T(8,128)(2,1)}, u32[]{:S(2)}, u32[]{:S(2)}) async-start(bf16[2,16,64,1024]{3,2,0,1:T(8,128)(2,1)} %copy.145), calls=%async_computation.5 | async-start | bytes 8388608 | tf_op jit(solution)/shard_map/all_to_all | solution.py:144
  494.3 260.2 %reduce-scatter.12.cloned.1.call-start = ((), (), s32[]{:S(2)}) async-start(), calls=%async_computation.21 | async-start | bytes 2359296 | tf_op jit(solution)/shard_map/reduce_scatter | solution.py:307
  500.3 898.9 %reduce-scatter.8.cloned.1.call-start = ((), (), s32[]{:S(2)}) async-start(), calls=%async_computation.19 | async-start | bytes 4227072 | tf_op jit(solution)/shard_map/reduce_scatter | solution.py:369
  551.9 16.8 copy-start.13
  551.9 16.8 copy-start.24
  567.3 4.4 copy-start.15
  574.3 13.0 copy-start.32
  577.7 16.9 all-to-all-start.6
  587.0 1461.0 %reduce-scatter.6.cloned.1.call-start = ((), (), s32[]{:S(2)}) async-start(), calls=%async_computation.18 | async-start | bytes 8454144 | tf_op jit(solution)/shard_map/reduce_scatter | solution.py:368
  607.2 4.8 copy-start.8
  607.2 4.8 copy-start.37
  624.2 4.8 copy-start.8
  624.2 4.8 copy-start.37
  624.7 4.3 copy-start.11
  635.0 14.7 copy-start.6
  635.0 14.7 copy-start.26
  635.1 14.7 copy-start.30
  655.7 104.5 %copy-start.27 = (f32[1024]{0:T(1024)S(1)}, f32[1024]{0:T(1024)}, u32[]{:S(2)}) copy-start(f32[1024]{0:T(1024)} %get-tuple-element.238) | copy-start | bytes 12292
  655.7 171.9 %copy-start.3 = (f32[128,1024]{1,0:T(8,128)S(1)}, f32[128,1024]{1,0:T(8,128)}, u32[]{:S(2)}) copy-start(f32[128,1024]{1,0:T(8,128)} %copy-done.2) | copy-start | bytes 1572868
  655.7 171.9 %copy-start.34 = (f32[128]{0:T(128)S(1)}, f32[128]{0:T(128)}, u32[]{:S(2)}) copy-start(f32[128]{0:T(128)} %get-tuple-element.308) | copy-start | bytes 1540
  (16 other events, 55.9 us)
Sparse Core Ops, SparseCore 0:
  11.2 69.4 all-gather.5
  83.7 62.8 all-gather.7
  148.2 22.6 all-gather.9
  213.3 26.1 all-gather.11
  283.2 24.0 all-gather.13
  467.1 182.5 all-reduce.8
  652.3 32.0 reduce-scatter.13
  686.9 32.5 reduce-scatter.9
  722.0 32.4 reduce-scatter.11
  757.4 641.8 reduce-scatter.7
  1402.2 645.6 reduce-scatter.5
where the time goes:
time: 2060 us; the launch traced here: 2050 us
  waiting for transfers between devices  1560 us (76%)
  blocking collectives  205 us (10%)
  matrix products  95 us (5%)
  local copies, waits for them, and re-layouts  90 us (4%)
  other arithmetic  53.4 us (3%)
  starting transfers between devices  36.4 us (2%)
    reduce_scatter x1, waiting for transfers between devices, local(): lax.psum_scatter(grad_qkv, ('seq', 'wshard'), scatter_dimension=0, tiled=...  649 us
    reduce_scatter x1, waiting for transfers between devices, local(): lax.psum_scatter(grad_out, ('seq', 'wshard'), scatter_dimension=0, tiled=...  571 us
    unnamed x2, blocking collectives  135 us
    all_to_all x1, waiting for transfers between devices, combine_rows(): lax.all_to_all(shaped, 'wshard', split_axis=1, concat_axis=0, tiled=True)  59.4 us
    all_to_all x1, waiting for transfers between devices, dispatch_rows(): lax.all_to_all(shaped, 'wshard', split_axis=0, concat_axis=2, tiled=True)  57.8 us
    all_to_all x1, waiting for transfers between devices, dispatch_grads(): lax.all_to_all(shaped, 'wshard', split_axis=0, concat_axis=2, tiled=True)  56.9 us
    all_gather x1, blocking collectives, local(): lax.all_gather(router, ('seq', 'wshard'), axis=0, tiled=True)  56.3 us
    all_to_all x1, waiting for transfers between devices, combine_grads(): lax.all_to_all(shaped, 'wshard', split_axis=1, concat_axis=0, tiled=True)  51.5 us
  transfers between devices with their start and end apart: 18, of which 11 were waited for; matrix products, arithmetic and copies ran while one was open for 10% of the time, Pallas kernels for 0%

commit v1 on v0

--- a/solution.py
+++ b/solution.py
@@ -108,41 +108,13 @@
     return (grad_queries.reshape(length, heads_dev, head_size), totals[0], totals[1])
 
 
-def route_slots(chosen_ids, experts_all):
-    flat_ids = chosen_ids.reshape(-1)
-    onehot = (flat_ids[:, None] == jnp.arange(experts_all, dtype=jnp.int32)[None, :]).astype(
-        jnp.int32
-    )
-    places = jnp.cumsum(onehot, axis=0) - 1
-    return (flat_ids, jnp.sum(places * onehot, axis=1))
-
-
-def dispatch_rows(buffer, owners):
-    experts_all, capacity, features = buffer.shape
-    shaped = buffer.reshape(owners, experts_all // owners, capacity, features)
-    arrived = lax.all_to_all(shaped, "wshard", split_axis=0, concat_axis=2, tiled=True)
-    return arrived.reshape(experts_all // owners, owners * capacity, features)
-
-
-def combine_rows(results, owners):
-    local_experts, received_rows, features = results.shape
-    shaped = results.reshape(local_experts, owners, received_rows // owners, features)
-    arrived = lax.all_to_all(shaped, "wshard", split_axis=1, concat_axis=0, tiled=True)
-    return arrived.reshape(local_experts * owners, received_rows // owners, features)
-
-
-def dispatch_grads(buffer, owners):
-    experts_all, capacity, features = buffer.shape
-    shaped = buffer.reshape(owners, experts_all // owners, capacity, features)
-    arrived = lax.all_to_all(shaped, "wshard", split_axis=0, concat_axis=2, tiled=True)
-    return arrived.reshape(experts_all // owners, owners * capacity, features)
-
-
-def combine_grads(results, owners):
-    local_experts, received_rows, features = results.shape
-    shaped = results.reshape(local_experts, owners, received_rows // owners, features)
-    arrived = lax.all_to_all(shaped, "wshard", split_axis=1, concat_axis=0, tiled=True)
-    return arrived.reshape(local_experts * owners, received_rows // owners, features)
+def dense_gates(logits, chosen_ids, experts_all):
+    named = jnp.any(
+        chosen_ids[..., None] == jnp.arange(experts_all, dtype=jnp.int32), axis=-2
+    )
+    peak = jnp.max(jnp.where(named, logits, -jnp.inf), axis=-1, keepdims=True)
+    exponent = jnp.where(named, jnp.exp(logits - peak), 0.0)
+    return (named, exponent / jnp.sum(exponent, axis=-1, keepdims=True))
 
 
 def norm_backward(grad_normed, values, scale, gain_full):
@@ -182,16 +154,25 @@
     query_width = HEADS * HEAD_DIM
     key_width = KV_HEADS * HEAD_DIM
     length = tok_dev * seq_parts
-    fetched = (
-        lax.all_gather(weight_qkv, ("seq", "wshard"), axis=0, tiled=True),
-        lax.all_gather(weight_out, ("seq", "wshard"), axis=0, tiled=True),
-        lax.all_gather(router, ("seq", "wshard"), axis=0, tiled=True),
-        lax.all_gather(gain_attn, ("seq", "wshard"), axis=0, tiled=True),
-        lax.all_gather(gain_ffn, ("seq", "wshard"), axis=0, tiled=True),
-    )
-    qkv_full, out_full, router_full = (fetched[0], fetched[1], fetched[2])
-    gain_one = fetched[3].astype(jnp.float32)
-    gain_two = fetched[4].astype(jnp.float32)
+    smalls = jnp.concatenate(
+        [
+            weight_out,
+            router,
+            gain_attn[:, None],
+            gain_ffn[:, None],
+            jnp.zeros((router.shape[0], 128 - experts_all - 2), jnp.bfloat16),
+        ],
+        axis=1,
+    )
+    gains = lax.all_gather(gain_attn, ("seq", "wshard"), axis=0, tiled=True)
+    qkv_full = lax.all_gather(weight_qkv, ("seq", "wshard"), axis=0, tiled=True)
+    smalls_full = lax.all_gather(smalls, ("seq", "wshard"), axis=0, tiled=True)
+    out_full = smalls_full[:, :features]
+    router_full = smalls_full[:, features : features + experts_all]
+    gain_one = gains.astype(jnp.float32)
+    gain_two = smalls_full[:, features + experts_all + 1].astype(jnp.float32)
+    ids_all = lax.all_gather(expert_ids[0], "wshard", axis=0)
+    cot_all = lax.all_gather(cotangent[0], "wshard", axis=0)
     owned = (
         lax.all_gather(expert_gate, "seq", axis=1, tiled=True),
         lax.all_gather(expert_up, "seq", axis=1, tiled=True),
@@ -239,14 +220,37 @@
     scale_two = rms_scale(hidden)
     normed_two = (hidden * scale_two * gain_two).astype(jnp.bfloat16)
     logits = jnp.dot(normed_two, router_full, preferred_element_type=jnp.float32)
-    chosen = jnp.take_along_axis(logits, chosen_ids, axis=1)
-    peak_logit = jnp.max(chosen, axis=1, keepdims=True)
-    exponent = jnp.exp(chosen - peak_logit)
-    gate_share = exponent / jnp.sum(exponent, axis=1, keepdims=True)
-    flat_ids, slot_of = route_slots(chosen_ids, experts_all)
-    buffer = jnp.zeros((experts_all, capacity, features), jnp.bfloat16)
-    buffer = buffer.at[flat_ids, slot_of].set(jnp.repeat(normed_two, top_count, axis=0))
-    received = dispatch_rows(buffer, owners)
+    _, gates_own = dense_gates(logits, chosen_ids, experts_all)
+    normed_all = lax.all_gather(normed_two, "wshard", axis=0)
+    logits_all = jnp.einsum(
+        "std,de->ste", normed_all, router_full, preferred_element_type=jnp.float32
+    )
+    named_all, gates_all = dense_gates(logits_all, ids_all, experts_all)
+    first_expert = lax.axis_index("wshard") * local_experts
+    named = lax.dynamic_slice_in_dim(named_all, first_expert, local_experts, axis=2)
+    gates_mine = lax.dynamic_slice_in_dim(gates_all, first_expert, local_experts, axis=2)
+    lower = jnp.tril(jnp.ones((tok_dev, tok_dev), jnp.bfloat16))
+    places = jnp.einsum(
+        "ut,ste->seu", lower, named.astype(jnp.bfloat16), preferred_element_type=jnp.float32
+    ).astype(jnp.int32) - 1
+    picks = (
+        places[:, :, None, :] == jnp.arange(capacity, dtype=jnp.int32)[None, None, :, None]
+    ) & jnp.transpose(named, (0, 2, 1))[:, :, None, :]
+    picks = jnp.transpose(picks, (1, 0, 2, 3))
+    pick = picks.astype(jnp.bfloat16)
+    row_gate = jnp.sum(
+        jnp.where(picks, jnp.transpose(gates_mine, (2, 0, 1))[:, :, None, :], 0.0), axis=-1
+    ).reshape(local_experts, owners * capacity)
+    received = (
+        jnp.einsum("esct,std->escd", pick, normed_all, preferred_element_type=jnp.float32)
+        .astype(jnp.bfloat16)
+        .reshape(local_experts, owners * capacity, features)
+    )
+    cot_rows = (
+        jnp.einsum("esct,std->escd", pick, cot_all, preferred_element_type=jnp.float32)
+        .astype(jnp.bfloat16)
+        .reshape(local_experts, owners * capacity, features)
+    )
     gate_val = jnp.einsum("erd,edf->erf", received, gate_full, preferred_element_type=jnp.float32)
     up_val = jnp.einsum("erd,edf->erf", received, up_full, preferred_element_type=jnp.float32)
     sigma = jax.nn.sigmoid(gate_val)
@@ -255,33 +259,33 @@
     produced = jnp.einsum(
         "erf,efd->erd", inner_act, down_full, preferred_element_type=jnp.float32
     ).astype(jnp.bfloat16)
-    returned = combine_rows(produced, owners)
-    routed = returned[flat_ids, slot_of].reshape(tok_dev, top_count, features)
-    mixture = jnp.sum(gate_share[:, :, None] * routed, axis=1)
-    output = hidden + residual_multiplier * mixture
+    grad_mix_rows = residual_multiplier * cot_rows.astype(jnp.float32)
+    weighted = (row_gate[:, :, None] * produced).astype(jnp.bfloat16)
+    mix_part = jnp.einsum(
+        "esct,escd->std",
+        pick,
+        weighted.reshape(local_experts, owners, capacity, features),
+        preferred_element_type=jnp.float32,
+    ).astype(jnp.bfloat16)
+    grad_gate_rows = jnp.sum(produced * grad_mix_rows, axis=-1).reshape(
+        local_experts, owners, capacity
+    )
+    gate_part = jnp.sum(
+        jnp.where(picks, grad_gate_rows[:, :, :, None], 0.0), axis=2
+    )
+    gate_part = jnp.transpose(gate_part, (1, 2, 0))
+    grad_gates = lax.all_to_all(gate_part, "wshard", split_axis=0, concat_axis=0, tiled=True)
+    grad_gates = jnp.transpose(grad_gates, (1, 0, 2)).reshape(tok_dev, experts_all)
+    mixture = lax.psum_scatter(mix_part, "wshard", scatter_dimension=0, tiled=True)[0]
+    output = hidden + residual_multiplier * mixture.astype(jnp.float32)
     grad_output = cotangent[0].astype(jnp.float32)
-    grad_mix = residual_multiplier * grad_output
-    grad_gates = jnp.sum(routed * grad_mix[:, None, :], axis=-1)
-    grad_chosen = gate_share * (
-        grad_gates - jnp.sum(gate_share * grad_gates, axis=1, keepdims=True)
-    )
-    onehot_route = (
-        chosen_ids[:, :, None] == jnp.arange(experts_all, dtype=jnp.int32)[None, None, :]
-    ).astype(jnp.float32)
-    grad_logits = jnp.einsum("tk,tke->te", grad_chosen, onehot_route).astype(jnp.bfloat16)
+    grad_logits = (
+        gates_own
+        * (grad_gates - jnp.sum(gates_own * grad_gates, axis=1, keepdims=True))
+    ).astype(jnp.bfloat16)
     grad_router = jnp.dot(normed_two.T, grad_logits, preferred_element_type=jnp.float32)
     grad_normed_two = jnp.dot(grad_logits, router_full.T, preferred_element_type=jnp.float32)
-    grad_routed = (
-        (gate_share[:, :, None] * grad_mix[:, None, :])
-        .astype(jnp.bfloat16)
-        .reshape(tok_dev * top_count, features)
-    )
-    grad_buffer = (
-        jnp.zeros((experts_all, capacity, features), jnp.bfloat16)
-        .at[flat_ids, slot_of]
-        .set(grad_routed)
-    )
-    grad_received = dispatch_grads(grad_buffer, owners)
+    grad_received = (row_gate[:, :, None] * grad_mix_rows).astype(jnp.bfloat16)
     grad_inner = jnp.einsum(
         "erd,efd->erf", grad_received, down_full, preferred_element_type=jnp.float32
     )
@@ -296,6 +300,13 @@
         jnp.einsum("erf,edf->erd", grad_gate_val, gate_full, preferred_element_type=jnp.float32)
         + jnp.einsum("erf,edf->erd", grad_up_val, up_full, preferred_element_type=jnp.float32)
     ).astype(jnp.bfloat16)
+    rows_part = jnp.einsum(
+        "esct,escd->std",
+        pick,
+        grad_rows.reshape(local_experts, owners, capacity, features),
+        preferred_element_type=jnp.float32,
+    ).astype(jnp.bfloat16)
+    grad_back = lax.psum_scatter(rows_part, "wshard", scatter_dimension=0, tiled=True)[0]
     grad_gate = jnp.einsum(
         "erd,erf->edf", received, grad_gate_val, preferred_element_type=jnp.float32
     )
@@ -311,11 +322,7 @@
             grad_down.astype(jnp.bfloat16), "seq", scatter_dimension=1, tiled=True
         ).astype(jnp.float32),
     )
-    grad_back = combine_grads(grad_rows, owners)
-    grad_normed_two = grad_normed_two + jnp.sum(
-        grad_back[flat_ids, slot_of].reshape(tok_dev, top_count, features).astype(jnp.float32),
-        axis=1,
-    )
+    grad_normed_two = grad_normed_two + grad_back.astype(jnp.float32)
     grad_hidden_norm, grad_gain_ffn = norm_backward(grad_normed_two, hidden, scale_two, gain_two)
     grad_hidden = grad_output + grad_hidden_norm
     grad_branch = (residual_multiplier * grad_hidden).astype(jnp.bfloat16)
@@ -364,12 +371,32 @@
     grad_normed_one = jnp.dot(grad_proj, qkv_full.T, preferred_element_type=jnp.float32)
     grad_input_norm, grad_gain_attn = norm_backward(grad_normed_one, inputs, scale_one, gain_one)
     grad_input = grad_hidden + grad_input_norm
+    packed_grads = jnp.concatenate(
+        [
+            grad_qkv,
+            grad_out,
+            grad_router,
+            grad_gain_attn[:, None],
+            grad_gain_ffn[:, None],
+            jnp.zeros((features, 128 - experts_all - 2), jnp.float32),
+        ],
+        axis=1,
+    ).astype(jnp.bfloat16)
+    width = packed_grads.shape[1]
+    by_owner = jnp.transpose(
+        packed_grads.reshape(seq_parts, owners, features // (seq_parts * owners), width),
+        (1, 0, 2, 3),
+    ).reshape(owners, features // owners, width)
+    by_seq = lax.psum_scatter(by_owner, "wshard", scatter_dimension=0, tiled=True)
+    by_seq = by_seq.reshape(seq_parts, features // (seq_parts * owners), width)
+    own = lax.psum_scatter(by_seq, "seq", scatter_dimension=0, tiled=True)[0].astype(jnp.float32)
+    qkv_cols = grad_qkv.shape[1]
     shares = (
-        lax.psum_scatter(grad_qkv, ("seq", "wshard"), scatter_dimension=0, tiled=True),
-        lax.psum_scatter(grad_out, ("seq", "wshard"), scatter_dimension=0, tiled=True),
-        lax.psum_scatter(grad_router, ("seq", "wshard"), scatter_dimension=0, tiled=True),
-        lax.psum_scatter(grad_gain_attn, ("seq", "wshard"), scatter_dimension=0, tiled=True),
-        lax.psum_scatter(grad_gain_ffn, ("seq", "wshard"), scatter_dimension=0, tiled=True),
+        own[:, :qkv_cols],
+        own[:, qkv_cols : qkv_cols + features],
+        own[:, qkv_cols + features : qkv_cols + features + experts_all],
+        own[:, qkv_cols + features + experts_all],
+        own[:, qkv_cols + features + experts_all + 1],
     )
     return (
         output.astype(jnp.bfloat16)[None],

time: 2060 us -> 855 us (0.42)
  waiting for transfers between devices: 1560 us -> 508 us
  blocking collectives: 205 us -> 90.9 us
  local copies, waits for them, and re-layouts: 90 us -> 66.1 us
    reduce_scatter x2 -> x0, waiting for transfers between devices: 1220 us -> none  [the longest x1 649 us: local(): lax.psum_scatter(grad_qkv, ('seq', 'wshard'), scatter_dimension=0, tiled=...]
    unnamed x12 -> x18, waiting for transfers between devices: 2.83 us -> 227 us
    all_to_all x4 -> x2, waiting for transfers between devices: 226 us -> 13.9 us  [the longest x1 7.56 us: local(): lax.all_to_all(gate_part, 'wshard', split_axis=0, concat_axis=0, tiled=True)]
    all_gather x2 -> x4, waiting for transfers between devices: 0.04 us -> 95.3 us  [the longest x1 46.3 us: local(): normed_all = lax.all_gather(normed_two, 'wshard', axis=0)]
    unnamed x2 -> x1, blocking collectives: 135 us -> 69.1 us
    gather x6 -> x0, local copies, waits for them, and re-layouts: 37.9 us -> none  [the longest x1 15.3 us: local(): grad_back[flat_ids, slot_of].reshape(tok_dev, top_count, features)]
    all_gather x1, blocking collectives: 56.3 us -> 21.8 us  [local(): ids_all = lax.all_gather(expert_ids[0], 'wshard', axis=0)]
  transfers between devices with their start and end apart: 18 -> 19, of which waited for: 11 -> 17; matrix products, arithmetic and copies ran while one was open for 10% -> 12% of each run, Pallas kernels for 0% -> 0%
where the time goes in v1:
time: 855 us; the launch traced here: 846 us
  waiting for transfers between devices  508 us (59%)
  matrix products  106 us (12%)
  blocking collectives  90.9 us (11%)
  local copies, waits for them, and re-layouts  66.1 us (8%)
  other arithmetic  36.9 us (4%)
  starting transfers between devices  22.5 us (3%)
  between operations  15.2 us (2%)
    unnamed x18, waiting for transfers between devices  227 us
    unnamed x1, blocking collectives  69.1 us
    all_gather x1, waiting for transfers between devices, local(): normed_all = lax.all_gather(normed_two, 'wshard', axis=0)  46.3 us
    reduce_scatter x1, waiting for transfers between devices, local(): lax.psum_scatter(grad_down.astype(jnp.bfloat16), 'seq', scatter_dimension...  35.3 us
    reduce_scatter x1, waiting for transfers between devices, local(): lax.psum_scatter(grad_gate.astype(jnp.bfloat16), 'seq', scatter_dimension...  33.2 us
    reduce_scatter x1, waiting for transfers between devices, local(): lax.psum_scatter(grad_up.astype(jnp.bfloat16), 'seq', scatter_dimension=1...  33.1 us
    all_gather x1, waiting for transfers between devices, local(): smalls_full = lax.all_gather(smalls, ('seq', 'wshard'), axis=0, tiled=True)  26.8 us
    all_gather x1, waiting for transfers between devices, local(): cot_all = lax.all_gather(cotangent[0], 'wshard', axis=0)  22.1 us
  transfers between devices with their start and end apart: 19, of which 17 were waited for; matrix products, arithmetic and copies ran while one was open for 12% of the time, Pallas kernels for 0%

profile of v1, /device:TPU:0, one launch (start us, length us, event | category | flops | bytes accessed | tf_op | source)
XLA Modules:
  0.0 846.5 jit_solution(9646788744705197014)
XLA Ops:
  12.5 69.1 %all-reduce = bf16[1024]{0:T(1024)(128)(2,1)S(1)} all-reduce(bf16[1024]{0:T(1024)(128)(2,1)S(1)} %dynamic-update-slice), channel_id=1, replica_groups=mesh['seq'=8,'wshard'=16] {'seq','wshard'}, use_global_device_ids=true, to_apply=%add | all-reduce | flops 1024 | bytes 4096
  83.8 3.1 fusion.142
  88.4 3.5 all-to-all-start
  91.9 10.3 %all-to-all-done = bf16[128,8,256]{0,2,1:T(8,128)(2,1)S(1)} async-done(((bf16[128,8,256]{0,2,1:T(8,128)(2,1)}), bf16[128,8,256]{0,2,1:T(8,128)(2,1)S(1)}, u32[]{:S(2)}, u32[]{:S(2)}) %all-to-all-start) | async-done | bytes 524320 | tf_op jit(solution)/shard_map/all_to_all | solution.py:203
  103.6 11.0 %while.28 = (s32[]{:T(128)}, bf16[2,512,128]{2,1,0:T(8,128)(2,1)S(1)}, f32[2,1,2,512]{3,2,1,0:T(2,128)S(1)}, s32[2]{0:T(128)S(1)}, bf16[2,512,1,2,64]{1,4,3,2,0:...) while((s32[]{:T(128)}, ...), condition=%wide.region_4.5_spmd.clone, body=%wide.region_1.4_spmd.clone.sunk | while | flops 281542144 | bytes 15765625 | solution.py:63
  116.7 3.4 all-to-all-start.1
  120.2 26.8 %all-gather.11.cloned.1.call-done = bf16[1024,1152]{1,0:T(8,128)(2,1)} async-done(((bf16[8,1152]{1,0:T(8,128)(2,1)}), bf16[1024,1152]{1,0:T(8,128)(2,1)}) %all-gather.11.cloned.1.call-update) | async-done | bytes 2359312 | tf_op jit(solution)/shard_map/all_gather | solution.py:169
  153.8 21.8 %all_gather.33 = s32[16,128,8]{1,2,0:T(8,128)S(1)} all-gather(s32[1,128,8]{1,2,0:T(8,128)S(1)} %copy-done.23), channel_id=1, replica_groups=mesh['seq'=8,'wshard'=16] {'wshard'}, dimensions={0}, use_global_device_ids=true | all-gather | bytes 69632 | tf_op jit(solution)/shard_map/all_gather | solution.py:174
  176.3 22.1 %all-gather.19.cloned.1.call-done = bf16[16,128,1024]{2,1,0:T(8,128)(2,1)} async-done(((bf16[1,128,1024]{2,1,0:T(8,128)(2,1)}), bf16[16,128,1024]{2,1,0:T(8,128)(2,1)}) %all-gather.19.cloned.1.call-update) | async-done | bytes 4194320 | tf_op jit(solution)/shard_map/all_gather | solution.py:175
  198.3 3.4 convert_bitcast_fusion
  201.8 4.1 copy.241
  205.8 46.3 %all-gather.21.cloned.1.call-done = bf16[2048,1024]{1,0:T(8,128)(2,1)} async-done(((bf16[128,1024]{1,0:T(8,128)(2,1)}), bf16[2048,1024]{1,0:T(8,128)(2,1)}) %all-gather.21.cloned.1.call-update) | async-done | bytes 4194320 | tf_op jit(solution)/shard_map/all_gather | solution.py:224
  252.2 3.4 convert_bitcast_fusion.1
  255.6 2.7 copy.239
  262.8 15.7 %all-gather.13.cloned.1.call-done = bf16[2,1024,512]{2,1,0:T(8,128)(2,1)} async-done(((bf16[2,128,512]{2,1,0:T(8,128)(2,1)}), bf16[2,1024,512]{2,1,0:T(8,128)(2,1)}) %all-gather.13.cloned.1.call-update) | async-done | bytes 2097168 | tf_op jit(solution)/shard_map/all_gather | solution.py:177
  278.5 7.2 fusion.163
  285.7 19.8 %all-gather.15.cloned.1.call-done = bf16[2,1024,512]{2,1,0:T(8,128)(2,1)} async-done(((bf16[2,128,512]{2,1,0:T(8,128)(2,1)}), bf16[2,1024,512]{2,1,0:T(8,128)(2,1)}) %all-gather.15.cloned.1.call-update) | async-done | bytes 2097168 | tf_op jit(solution)/shard_map/all_gather | solution.py:178
  305.5 9.4 %multiply_convert_fusion.2 = (bf16[2,1024,512]{2,1,0:T(8,128)(2,1)}, f32[2,1024,512]{2,1,0:T(8,128)}) fusion(f32[2,1024,512]{2,1,0:T(8,128)} %fusion.163, bf16[2,1024,1024]{2,1,0:T(8,128)(2,1)} %bitcast.396, bf16[2,1024,512]{2,1,0:T(8,128)(2,1)} %all-gather.15.cloned.1.call-done), kind=kOutput, calls=%fused_computation.85 | convolution fusion | flops 2153775104 | bytes 16777216 | tf_op jit(solution)/shard_map/erd,edf->erf/dot_general | solution.py:255
  314.9 17.8 %all-gather.17.cloned.1.call-done = bf16[2,512,1024]{2,1,0:T(8,128)(2,1)} async-done(((bf16[2,64,1024]{2,1,0:T(8,128)(2,1)}), bf16[2,512,1024]{2,1,0:T(8,128)(2,1)}) %all-gather.17.cloned.1.call-update) | async-done | bytes 2097168 | tf_op jit(solution)/shard_map/all_gather | solution.py:179
  332.7 9.0 %fusion.58 = (f32[2,1024]{1,0:T(2,128)S(1)}, bf16[2,1024,1024]{2,1,0:T(8,128)(2,1)}) fusion(f32[2,16,64,1024]{3,2,1,0:T(8,128)} %copy.241, bf16[2,1024,512]{2,1,0:T(8,128)(2,1)} %get-tuple-element.327, bf16[2,512,1024]{2,1,0:T(8,128)(2,1)} %all-gather.17.cloned.1.call-done), kind=kOutput, calls=%fused_computation.68 | convolution fusion | flops 2157967360 | bytes 16785408 | tf_op jit(solution)/shard_map/erf,efd->erd/dot_general | solution.py:259
  343.1 4.0 fusion.59
  348.6 5.9 multiply_convert_fusion
  360.1 3.2 bitcast_convert_fusion
  363.4 2.9 fusion.57
  366.3 3.3 bitcast_convert_fusion.1
  371.7 7.0 all-to-all-start.2
  378.8 7.6 all-to-all-done.2
  386.4 55.3 %reduce-scatter.24.cloned.1.call-done = bf16[1,128,1024]{2,1,0:T(8,128)(2,1)} async-done(((bf16[16,128,1024]{2,1,0:T(8,128)(2,1)}), bf16[1,128,1024]{2,1,0:T(8,128)(2,1)}) %reduce-scatter.24.cloned.1.call-update) | async-done | bytes 262160
  443.1 79.2 %reduce-scatter.22.cloned.1.call-done = bf16[1,128,1024]{2,1,0:T(8,128)(2,1)} async-done(((bf16[16,128,1024]{2,1,0:T(8,128)(2,1)}), bf16[1,128,1024]{2,1,0:T(8,128)(2,1)}) %reduce-scatter.22.cloned.1.call-update) | async-done | bytes 262160
  527.4 4.5 all-to-all-start.3
  532.5 7.0 all-to-all-done.3
  539.8 23.2 %while.29 = (s32[]{:T(128)}, f32[1024,1,64]{0,2,1:T(8,128)S(1)}, f32[1024,1,64]{0,2,1:T(8,128)}, f32[2,512,2,64]{1,0,3,2:T(2,128)}, bf16[2,512,1,2,64]{1,4,3,2,0...) while((s32[]{:T(128)}, f32[1024,1,64]{0,2,1:T(8,128)S(1)}, ...), condition=%wide.region_21.22_spmd.clone, body=%wide.region_19.21_spmd.clone.sunk | while | flops 687734272 | bytes 43155740 | solution.py:105
  548.2 2.4 dynamic_update_slice.22
  559.7 2.4 dynamic_update_slice.22
  568.3 3.5 all-to-all-start.4
  575.7 6.4 all-to-all-done.4
  591.5 3.8 fusion.106
  598.1 4.2 convolution_convert_fusion
  602.4 10.4 %concatenate.54 = bf16[8,16,8,3200]{3,2,1,0:T(8,128)(2,1)} concatenate(bf16[8,16,8,2048]{3,2,1,0:T(8,128)(2,1)} %convolution_convert_fusion, bf16[8,16,8,1024]{3,2,1,0:T(8,128)(2,1)S(1)} %convolution_convert_fusion.5, bf16[8,16,8,32]{3,2,1,0:T(8,128)(2,1)S(1)} %bitcast.406, bf16[8,16,8,1]{3,2,1,0:T(8,128)(2,1)S(1)} %concatenate.55, bf16[8,16,8,1]{3,2,1,0:T(8,128)(2,1)S(1)} %copy-done.13, ...), dimensions={3} | concatenate | bytes 13107200 | tf_op jit(solution)/shard_map/concatenate | solution.py:374
  612.7 6.5 copy_bitcast_fusion
  620.8 5.9 convolution_convert_fusion.2
  626.8 6.8 convolution_convert_fusion.3
  633.7 5.9 convolution_convert_fusion.4
  639.7 59.1 %reduce-scatter.26.cloned.1.call-done = bf16[1,64,3200]{2,1,0:T(8,128)(2,1)} async-done(((bf16[16,64,3200]{2,1,0:T(8,128)(2,1)}), bf16[1,64,3200]{2,1,0:T(8,128)(2,1)}) %reduce-scatter.26.cloned.1.call-update) | async-done | bytes 409616
  698.9 35.3 %reduce-scatter.20.cloned.1.call-done = bf16[2,64,1024]{2,1,0:T(8,128)(2,1)} async-done(((bf16[2,512,1024]{2,1,0:T(8,128)(2,1)}), bf16[2,64,1024]{2,1,0:T(8,128)(2,1)}) %reduce-scatter.20.cloned.1.call-update) | async-done | bytes 262160 | tf_op jit(solution)/shard_map/reduce_scatter | solution.py:321
  735.9 33.1 %reduce-scatter.18.cloned.1.call-done = bf16[2,128,512]{2,1,0:T(8,128)(2,1)} async-done(((bf16[2,1024,512]{2,1,0:T(8,128)(2,1)}), bf16[2,128,512]{2,1,0:T(8,128)(2,1)}) %reduce-scatter.18.cloned.1.call-update) | async-done | bytes 262160 | tf_op jit(solution)/shard_map/reduce_scatter | solution.py:318
  770.8 33.2 %reduce-scatter.16.cloned.1.call-done = bf16[2,128,512]{2,1,0:T(8,128)(2,1)} async-done(((bf16[2,1024,512]{2,1,0:T(8,128)(2,1)}), bf16[2,128,512]{2,1,0:T(8,128)(2,1)}) %reduce-scatter.16.cloned.1.call-update) | async-done | bytes 262160 | tf_op jit(solution)/shard_map/reduce_scatter | solution.py:315
  805.8 30.3 %reduce-scatter.28.cloned.1.call-done = bf16[1,8,3200]{2,1,0:T(8,128)(2,1)} async-done(((bf16[8,8,3200]{2,1,0:T(8,128)(2,1)}), bf16[1,8,3200]{2,1,0:T(8,128)(2,1)}) %reduce-scatter.28.cloned.1.call-update) | async-done | bytes 51216
  (245 shorter events, 102.7 us)
Async XLA Ops:
  7.2 76.3 %all-gather.9.cloned.1.call-start = ((), (), s32[]{:S(2)}) async-start(), calls=%async_computation.12 | async-start | bytes 4227072 | tf_op jit(solution)/shard_map/all_gather | solution.py:168
  7.9 139.1 %all-gather.11.cloned.1.call-start = ((), (), s32[]{:S(2)}) async-start(), calls=%async_computation.13 | async-start | bytes 2377728 | tf_op jit(solution)/shard_map/all_gather | solution.py:169
  10.9 187.5 %all-gather.19.cloned.1.call-start = ((), (), s32[]{:S(2)}) async-start(), calls=%async_computation.17 | async-start | bytes 4456448 | tf_op jit(solution)/shard_map/all_gather | solution.py:175
  81.7 1.8 copy-start.21
  88.4 13.9 %all-to-all-start = ((bf16[128,8,256]{0,2,1:T(8,128)(2,1)}), bf16[128,8,256]{0,2,1:T(8,128)(2,1)S(1)}, u32[]{:S(2)}, u32[]{:S(2)}) async-start(bf16[128,8,256]{0,2,1:T(8,128)(2,1)} %pad_maximum_fusion), calls=%async_computation | async-start | bytes 1048576 | tf_op jit(solution)/shard_map/all_to_all | solution.py:203
  103.6 45.1 %copy-start.3 = (bf16[1,128,1024]{2,1,0:T(8,128)(2,1)S(1)}, bf16[1,128,1024]{2,1,0:T(8,128)(2,1)}, u32[]{:S(2)}) copy-start(bf16[1,128,1024]{2,1,0:T(8,128)(2,1)} %param.15) | copy-start | bytes 786436
  115.9 37.9 %copy-start.23 = (s32[1,128,8]{1,2,0:T(8,128)S(1)}, s32[1,128,8]{1,2,0:T(8,128)}, u32[]{:S(2)}) copy-start(s32[1,128,8]{1,2,0:T(8,128)} %param.24) | copy-start | bytes 12292
  116.7 31.5 %all-to-all-start.1 = ((bf16[8,2,8192]{2,1,0:T(2,128)(2,1)}), bf16[8,2,8192]{2,1,0:T(2,128)(2,1)S(1)}, u32[]{:S(2)}, u32[]{:S(2)}) async-start(bf16[8,2,8192]{2,1,0:T(2,128)(2,1)} %reshape.550), calls=%async_computation.1 | async-start | bytes 524288 | tf_op jit(solution)/shard_map/all_to_all | solution.py:210
  120.1 132.1 %all-gather.21.cloned.1.call-start = ((), (), s32[]{:S(2)}) async-start(), calls=%async_computation.21 | async-start | bytes 4456448 | tf_op jit(solution)/shard_map/all_gather | solution.py:224
  148.7 53.1 %copy-start.15 = (bf16[128,8,1,128]{0,3,1,2:T(8,128)(2,1)}, bf16[128,8,1,128]{0,3,1,2:T(8,128)(2,1)S(1)}, u32[]{:S(2)}) copy-start(bf16[128,8,1,128]{0,3,1,2:T(8,128)(2,1)S(1)} %copy.231) | copy-start | bytes 786436
  151.8 126.6 %all-gather.13.cloned.1.call-start = ((), (), s32[]{:S(2)}) async-start(), calls=%async_computation.14 | async-start | bytes 2359296 | tf_op jit(solution)/shard_map/all_gather | solution.py:177
  152.4 153.0 %all-gather.15.cloned.1.call-start = ((), (), s32[]{:S(2)}) async-start(), calls=%async_computation.15 | async-start | bytes 2359296 | tf_op jit(solution)/shard_map/all_gather | solution.py:178
  153.0 179.6 %all-gather.17.cloned.1.call-start = ((), (), s32[]{:S(2)}) async-start(), calls=%async_computation.16 | async-start | bytes 2359296 | tf_op jit(solution)/shard_map/all_gather | solution.py:179
  153.8 287.9 %reduce-scatter.24.cloned.1.call-start = ((), (), s32[]{:S(2)}) async-start(), calls=%async_computation.23 | async-start | bytes 4456448
  255.6 3.7 copy-start
  343.1 4.1 copy-start.10
  343.1 5.6 copy-start.27
  347.1 7.4 copy-start.2
  348.6 5.9 copy-start.6
  354.6 2.4 copy-start.4
  354.6 2.4 copy-start.8
  354.6 3.1 copy-start.9
  363.3 159.0 %reduce-scatter.22.cloned.1.call-start = ((), (), s32[]{:S(2)}) async-start(), calls=%async_computation.22 | async-start | bytes 4456448
  369.6 0.9 copy-start.1
  369.6 152.7 %copy-start.12 = (bf16[1,128,1024]{2,1,0:T(8,128)(2,1)S(1)}, bf16[1,128,1024]{2,1,0:T(8,128)(2,1)}, u32[]{:S(2)}) copy-start(bf16[1,128,1024]{2,1,0:T(8,128)(2,1)} %param.25) | copy-start | bytes 786436
  371.7 14.6 %all-to-all-start.2 = ((f32[16,128,2]{1,2,0:T(2,128)}), f32[16,128,2]{1,2,0:T(2,128)S(1)}, u32[]{:S(2)}, u32[]{:S(2)}) async-start(f32[16,128,2]{1,2,0:T(2,128)} %bitcast.35), calls=%async_computation.2 | async-start | bytes 32768 | tf_op jit(solution)/shard_map/all_to_all | solution.py:277
  527.4 12.0 %all-to-all-start.3 = ((bf16[128,8,128]{0,2,1:T(8,128)(2,1)}), bf16[128,8,128]{0,2,1:T(8,128)(2,1)S(1)}, u32[]{:S(2)}, u32[]{:S(2)}) async-start(bf16[128,8,128]{0,2,1:T(8,128)(2,1)} %bitcast.43), calls=%async_computation.3 | async-start | bytes 524288 | tf_op jit(solution)/shard_map/all_to_all | solution.py:333
  539.8 2.4 copy-start.19
  543.5 1.7 copy-start.20
  546.6 1.6 copy-start.17
  550.6 0.8 copy-start.18
  551.4 2.4 copy-start.19
  555.1 1.7 copy-start.20
  558.1 1.6 copy-start.17
  568.3 13.8 %all-to-all-start.4 = ((bf16[8,2,16384]{2,1,0:T(2,128)(2,1)}), bf16[8,2,16384]{2,1,0:T(2,128)(2,1)S(1)}, u32[]{:S(2)}, u32[]{:S(2)}) async-start(bf16[8,2,16384]{2,1,0:T(2,128)(2,1)} %reshape.552), calls=%async_computation.4 | async-start | bytes 1048576 | tf_op jit(solution)/shard_map/all_to_all | solution.py:355
  571.8 127.0 %reduce-scatter.26.cloned.1.call-start = ((), (), s32[]{:S(2)}) async-start(), calls=%async_computation.24 | async-start | bytes 6963200
  574.0 17.5 %copy-start.22 = (f32[1024]{0:T(1024)S(1)}, f32[1024]{0:T(1024)}, u32[]{:S(2)}) copy-start(f32[1024]{0:T(1024)} %copy-done.21) | copy-start | bytes 12292
  574.0 17.5 %copy-start.25 = (f32[128]{0:T(128)S(1)}, f32[128]{0:T(128)}, u32[]{:S(2)}) copy-start(f32[128]{0:T(128)} %copy-done.24) | copy-start | bytes 1540
  585.5 5.4 copy-start.14
  585.5 9.9 %copy-start.26 = (f32[128]{0:T(128)S(1)}, f32[128]{0:T(128)}, u32[]{:S(2)}) copy-start(f32[128]{0:T(128)} %get-tuple-element.321) | copy-start | bytes 1540
  595.4 7.0 copy-start.11
  595.4 7.0 copy-start.13
  619.2 1.6 copy-start.7
  619.3 114.9 %reduce-scatter.20.cloned.1.call-start = ((), (), s32[]{:S(2)}) async-start(), calls=%async_computation.20 | async-start | bytes 2359296 | tf_op jit(solution)/shard_map/reduce_scatter | solution.py:321
  626.8 6.9 copy-start.5
  626.8 142.2 %reduce-scatter.18.cloned.1.call-start = ((), (), s32[]{:S(2)}) async-start(), calls=%async_computation.19 | async-start | bytes 2359296 | tf_op jit(solution)/shard_map/reduce_scatter | solution.py:318
  633.6 170.4 %reduce-scatter.16.cloned.1.call-start = ((), (), s32[]{:S(2)}) async-start(), calls=%async_computation.18 | async-start | bytes 2359296 | tf_op jit(solution)/shard_map/reduce_scatter | solution.py:315
  639.7 196.5 %reduce-scatter.28.cloned.1.call-start = ((), (), s32[]{:S(2)}) async-start(), calls=%async_computation.25 | async-start | bytes 460800
  (3 other events, 2.0 us)
Sparse Core Ops, SparseCore 0:
  11.2 69.4 all-gather.8
  84.2 62.7 all-gather.10
  149.1 49.1 all-gather.18
  200.9 51.2 all-gather.20
  253.7 24.6 all-gather.12
  280.0 25.4 all-gather.14
  307.2 25.4 all-gather.16
  363.5 78.1 reduce-scatter.23
  445.4 76.8 reduce-scatter.21
  619.4 79.3 reduce-scatter.25
  701.4 32.7 reduce-scatter.19
  736.5 32.4 reduce-scatter.17
  771.5 32.4 reduce-scatter.15
  806.4 29.6 reduce-scatter.27

commit v2 on v1

--- a/solution.py
+++ b/solution.py
@@ -1,6 +1,8 @@
 import jax
 import jax.numpy as jnp
 from jax import lax
+from jax.experimental import pallas as pl
+from jax.experimental.pallas import tpu as pltpu
 from jax.sharding import PartitionSpec as P
 
 HEADS = 16
@@ -12,6 +14,518 @@
 attention_multiplier = 0.015625
 residual_multiplier = 0.22
 rope_theta = 10000.0
+
+
+MESH = pl.DeviceIdType.MESH
+SIDE = 4
+
+
+def plane_place(first, offset_first, offset_second):
+    mine = lax.axis_index("wshard")
+    z, y = mine // SIDE, mine % SIDE
+    if first == "y":
+        return ((z + offset_second + SIDE) % SIDE, (y + offset_first + SIDE) % SIDE)
+    return ((z + offset_first + SIDE) % SIDE, (y + offset_second + SIDE) % SIDE)
+
+
+def plane_peer(first, offset_first, offset_second):
+    z, y = plane_place(first, offset_first, offset_second)
+    return {"wshard": z * SIDE + y}
+
+
+def plane_neighbours():
+    return [plane_peer("y", step, 0) for step in (1, -1)] + [
+        plane_peer("y", 0, step) for step in (1, -1)
+    ]
+
+
+def seq_peer(offset_x, flip):
+    mine = lax.axis_index("seq")
+    x, core = mine // 2, mine % 2
+    if flip:
+        core = 1 - core
+    return {"seq": ((x + offset_x) % SIDE) * 2 + core}
+
+
+def greet(peers):
+    barrier = pltpu.get_barrier_semaphore()
+    for peer in peers:
+        pl.semaphore_signal(barrier, inc=1, device_id=peer, device_id_type=MESH)
+    pl.semaphore_wait(barrier, len(peers))
+
+
+HALVES = (("y", 0), ("z", 2))
+ORDER = (0, -1, 1, 2)
+
+
+def plane_gather(own, view, send, recv, after_row):
+    started = []
+
+    def copy(half, kind, source, target, peer):
+        return pltpu.make_async_remote_copy(
+            src_ref=source,
+            dst_ref=target,
+            send_sem=send.at[half, kind],
+            recv_sem=recv.at[half, kind],
+            device_id=peer,
+            device_id_type=MESH,
+        )
+
+    def push(half, kind, source, target, peer):
+        item = copy(half, kind, source, target, peer)
+        item.start()
+        started.append(item)
+
+    def arrived(half, kind, target):
+        first, _ = HALVES[half]
+        copy(half, kind, target, target, plane_peer(first, 1, 0)).wait_recv()
+
+    def block(half, along_first, along_second, low, count):
+        first, base = HALVES[half]
+        z, y = plane_place(first, along_first, along_second)
+        return view(z, y, base + low, count)
+
+    def ring(half, slot, axis, along, source):
+        first, base = HALVES[half]
+        for kind, step in ((0, 1), (1, -1)):
+            peer = plane_peer(first, step, 0) if axis == 0 else plane_peer(first, 0, step)
+            push(half, 4 * slot + kind, source, block(half, along, 0, 0, 2), peer)
+
+    def ring_relay(half, slot, axis, along):
+        first, base = HALVES[half]
+        for kind, step in ((0, 1), (1, -1)):
+            where = (-step, 0) if axis == 0 else (along, -step)
+            arrived(half, 4 * slot + kind, block(half, where[0], where[1], 0, 2))
+            part = block(half, where[0], where[1], kind, 1)
+            peer = plane_peer(first, step, 0) if axis == 0 else plane_peer(first, 0, step)
+            push(half, 4 * slot + 2 + kind, part, part, peer)
+
+    def ring_end(half, slot, axis, along):
+        where = (2, 0) if axis == 0 else (along, 2)
+        for kind in (0, 1):
+            arrived(half, 4 * slot + 2 + kind, block(half, where[0], where[1], kind, 1))
+
+    for half in (0, 1):
+        ring(half, 0, 0, 0, own(HALVES[half][1], 2))
+    for half in (0, 1):
+        ring(half, 1, 1, 0, own(HALVES[half][1], 2))
+    for half in (0, 1):
+        ring_relay(half, 0, 0, 0)
+        for slot in (1, 2):
+            ring(half, 1 + slot, 1, ORDER[slot], block(half, ORDER[slot], 0, 0, 2))
+    for half in (0, 1):
+        ring_end(half, 0, 0, 0)
+        ring(half, 4, 1, 2, block(half, 2, 0, 0, 2))
+        after_row(half, 0)
+    for slot in (0, 1, 2, 3):
+        for half in (0, 1):
+            ring_relay(half, 1 + slot, 1, ORDER[slot])
+    for half in (0, 1):
+        after_row(half, -1)
+        after_row(half, 1)
+    for half in (0, 1):
+        for slot in (0, 1, 2, 3):
+            ring_end(half, 1 + slot, 1, ORDER[slot])
+        after_row(half, 2)
+    for item in started:
+        item.wait_send()
+
+
+def plane_reduce(parts, far, near, far_last, near_last, send, recv, store):
+    started = []
+
+    def copy(half, kind, source, target, peer):
+        return pltpu.make_async_remote_copy(
+            src_ref=source,
+            dst_ref=target,
+            send_sem=send.at[half, kind],
+            recv_sem=recv.at[half, kind],
+            device_id=peer,
+            device_id_type=MESH,
+        )
+
+    def push(half, kind, source, target, peer):
+        item = copy(half, kind, source, target, peer)
+        item.start()
+        started.append(item)
+
+    def arrived(half, kind, target):
+        first, _ = HALVES[half]
+        copy(half, kind, target, target, plane_peer(first, 1, 0)).wait_recv()
+
+    def rows(half, offset, low, count):
+        first, base = HALVES[half]
+        z, y = plane_place(first, 0, offset)
+        if first == "y":
+            return parts.at[z, :, pl.ds(base + low, count)]
+        return parts.at[:, y, pl.ds(base + low, count)]
+
+    def one(half, offset, low, count):
+        first, base = HALVES[half]
+        z, y = plane_place(first, offset, 0)
+        return parts.at[z, y, pl.ds(base + low, count)]
+
+    def add(target, *others):
+        total = target[...].astype(jnp.float32)
+        for other in others:
+            total = total + other[...].astype(jnp.float32)
+        target[...] = total.astype(target.dtype)
+
+    def add_rows(half, offset, low, count, *others):
+        target = rows(half, offset, low, count)
+        def step(at, carry):
+            add(target.at[at], *[other.at[at] for other in others])
+            return carry
+        lax.fori_loop(0, SIDE, step, 0)
+
+    def peer(half, axis, step):
+        first, _ = HALVES[half]
+        return plane_peer(first, 0, step) if axis == 1 else plane_peer(first, step, 0)
+
+    for half in (0, 1):
+        push(half, 0, rows(half, 2, 0, 1), far.at[half, 0], peer(half, 1, 1))
+        push(half, 1, rows(half, 2, 1, 1), far.at[half, 1], peer(half, 1, -1))
+    for half in (0, 1):
+        push(half, 2, rows(half, 1, 1, 1), near.at[half, 0, :, pl.ds(1, 1)], peer(half, 1, 1))
+        push(half, 3, rows(half, -1, 0, 1), near.at[half, 1, :, pl.ds(0, 1)], peer(half, 1, -1))
+    for half in (0, 1):
+        arrived(half, 0, far.at[half, 0])
+        add_rows(half, 1, 0, 1, far.at[half, 0])
+        push(half, 4, rows(half, 1, 0, 1), near.at[half, 0, :, pl.ds(0, 1)], peer(half, 1, 1))
+        arrived(half, 1, far.at[half, 1])
+        add_rows(half, -1, 1, 1, far.at[half, 1])
+        push(half, 5, rows(half, -1, 1, 1), near.at[half, 1, :, pl.ds(1, 1)], peer(half, 1, -1))
+    for half in (0, 1):
+        arrived(half, 2, near.at[half, 0, :, pl.ds(1, 1)])
+        arrived(half, 3, near.at[half, 1, :, pl.ds(0, 1)])
+        arrived(half, 4, near.at[half, 0, :, pl.ds(0, 1)])
+        arrived(half, 5, near.at[half, 1, :, pl.ds(1, 1)])
+        add_rows(half, 0, 0, 2, near.at[half, 0], near.at[half, 1])
+        push(half, 6, one(half, 2, 0, 1), far_last.at[half, 0], peer(half, 0, 1))
+        push(half, 7, one(half, 2, 1, 1), far_last.at[half, 1], peer(half, 0, -1))
+        push(half, 8, one(half, 1, 1, 1), near_last.at[half, 0, pl.ds(1, 1)], peer(half, 0, 1))
+        push(half, 9, one(half, -1, 0, 1), near_last.at[half, 1, pl.ds(0, 1)], peer(half, 0, -1))
+    for half in (0, 1):
+        arrived(half, 6, far_last.at[half, 0])
+        add(one(half, 1, 0, 1), far_last.at[half, 0])
+        push(half, 10, one(half, 1, 0, 1), near_last.at[half, 0, pl.ds(0, 1)], peer(half, 0, 1))
+        arrived(half, 7, far_last.at[half, 1])
+        add(one(half, -1, 1, 1), far_last.at[half, 1])
+        push(half, 11, one(half, -1, 1, 1), near_last.at[half, 1, pl.ds(1, 1)], peer(half, 0, -1))
+    for half in (0, 1):
+        arrived(half, 8, near_last.at[half, 0, pl.ds(1, 1)])
+        arrived(half, 9, near_last.at[half, 1, pl.ds(0, 1)])
+        arrived(half, 10, near_last.at[half, 0, pl.ds(0, 1)])
+        arrived(half, 11, near_last.at[half, 1, pl.ds(1, 1)])
+        total = one(half, 0, 0, 2)[...].astype(jnp.float32)
+        for side in (0, 1):
+            total = total + near_last[half, side].astype(jnp.float32)
+        store(HALVES[half][1], total)
+    for item in started:
+        item.wait_send()
+
+
+def reduce_scratch(quarter_rows, width):
+    unit = (quarter_rows, width)
+    return [
+        pltpu.VMEM((SIDE, SIDE, 4) + unit, jnp.bfloat16),
+        pltpu.VMEM((2, 2, SIDE, 1) + unit, jnp.bfloat16),
+        pltpu.VMEM((2, 2, SIDE, 2) + unit, jnp.bfloat16),
+        pltpu.VMEM((2, 2, 1) + unit, jnp.bfloat16),
+        pltpu.VMEM((2, 2, 2) + unit, jnp.bfloat16),
+        pltpu.SemaphoreType.DMA((2, 12)),
+        pltpu.SemaphoreType.DMA((2, 12)),
+    ]
+
+
+def comm_params(number, limit_mb):
+    return pltpu.CompilerParams(
+        collective_id=number, has_side_effects=True, vmem_limit_bytes=limit_mb * 1024 * 1024
+    )
+
+
+def nothing(half, offset):
+    return None
+
+
+def token_gather(block, number):
+    rows, width = block.shape
+
+    def kernel(own_ref, out_ref, send, recv, local_sem):
+        greet(plane_neighbours())
+        z, y = plane_place("y", 0, 0)
+        keep = pltpu.make_async_copy(own_ref, out_ref.at[z, y], local_sem)
+        keep.start()
+        plane_gather(
+            lambda low, count: own_ref.at[pl.ds(low, count)],
+            lambda z, y, low, count: out_ref.at[z, y, pl.ds(low, count)],
+            send,
+            recv,
+            nothing,
+        )
+        keep.wait()
+
+    out = pl.pallas_call(
+        kernel,
+        out_shape=jax.ShapeDtypeStruct((SIDE, SIDE, 4, rows // 4, width), block.dtype),
+        in_specs=[pl.BlockSpec(memory_space=pl.ANY)],
+        out_specs=pl.BlockSpec(memory_space=pl.ANY),
+        scratch_shapes=[
+            pltpu.SemaphoreType.DMA((2, 20)),
+            pltpu.SemaphoreType.DMA((2, 20)),
+            pltpu.SemaphoreType.DMA,
+        ],
+        compiler_params=comm_params(number, 8),
+        name="token_gather",
+    )(block.reshape(4, rows // 4, width))
+    return out.reshape(SIDE * SIDE, rows, width)
+
+
+def token_reduce(pieces, number):
+    owners, rows, _ = pieces[0].shape
+    widths = [piece.shape[2] for piece in pieces]
+    width = sum(widths)
+    quarter = rows // 4
+
+    def kernel(*refs):
+        ins, out_ref, rest = refs[: len(widths)], refs[len(widths)], refs[len(widths) + 1 :]
+        parts, far, near, far_last, near_last, send, recv, load = rest
+        loads, at = [], 0
+        for i, one_width in enumerate(widths):
+            loads.append(
+                pltpu.make_async_copy(
+                    ins[i], parts.at[:, :, :, :, pl.ds(at, one_width)], load.at[i]
+                )
+            )
+            loads[-1].start()
+            at += one_width
+        greet(plane_neighbours())
+        for item in loads:
+            item.wait()
+
+        def store(low, total):
+            out_ref[pl.ds(low, 2)] = total
+
+        plane_reduce(parts, far, near, far_last, near_last, send, recv, store)
+
+    out = pl.pallas_call(
+        kernel,
+        out_shape=jax.ShapeDtypeStruct((4, quarter, width), jnp.float32),
+        in_specs=[pl.BlockSpec(memory_space=pl.ANY)] * len(widths),
+        out_specs=pl.BlockSpec(memory_space=pltpu.VMEM),
+        scratch_shapes=reduce_scratch(quarter, width) + [pltpu.SemaphoreType.DMA((len(widths),))],
+        compiler_params=comm_params(number, 32),
+        name="token_reduce",
+    )(*[piece.reshape(SIDE, SIDE, 4, quarter, piece.shape[2]) for piece in pieces])
+    return out.reshape(rows, width)
+
+
+def weights_gather(piece, number):
+    rows, width = piece.shape
+
+    def kernel(own_ref, out_ref, send, recv, x_send, x_recv, core_send, core_recv, local_sem):
+        seq = lax.axis_index("seq")
+        x, core = seq // 2, seq % 2
+        x_peers = [seq_peer(step, False) for step in (1, 3, 2)]
+        other = seq_peer(0, True)
+        greet(plane_neighbours() + x_peers + [other])
+        z, y = plane_place("y", 0, 0)
+        keep = pltpu.make_async_copy(own_ref, out_ref.at[x, core, z, y], local_sem)
+        keep.start()
+        sends = []
+        for i, step in enumerate((1, 3, 2)):
+            item = pltpu.make_async_remote_copy(
+                src_ref=own_ref,
+                dst_ref=out_ref.at[x, core, z, y],
+                send_sem=x_send.at[i],
+                recv_sem=x_recv.at[i],
+                device_id=x_peers[i],
+                device_id_type=MESH,
+            )
+            item.start()
+            sends.append(item)
+        keep.wait()
+        for i, step in enumerate((1, 3, 2)):
+            came = out_ref.at[(x + SIDE - step) % SIDE, core, z, y]
+            pltpu.make_async_remote_copy(
+                src_ref=came,
+                dst_ref=came,
+                send_sem=x_send.at[i],
+                recv_sem=x_recv.at[i],
+                device_id=x_peers[i],
+                device_id_type=MESH,
+            ).wait_recv()
+
+        swaps = []
+
+        def swap(half, offset):
+            first, base = HALVES[half]
+            z, y = plane_place(first, 0, offset)
+            mine = (
+                out_ref.at[pl.ds(base, 2), core, z]
+                if first == "y"
+                else out_ref.at[pl.ds(base, 2), core, :, y]
+            )
+            theirs = (
+                out_ref.at[pl.ds(base, 2), 1 - core, z]
+                if first == "y"
+                else out_ref.at[pl.ds(base, 2), 1 - core, :, y]
+            )
+            kind = ORDER.index(offset)
+            item = pltpu.make_async_remote_copy(
+                src_ref=mine,
+                dst_ref=mine,
+                send_sem=core_send.at[half, kind],
+                recv_sem=core_recv.at[half, kind],
+                device_id=other,
+                device_id_type=MESH,
+            )
+            item.start()
+            sends.append(item)
+            swaps.append(
+                pltpu.make_async_remote_copy(
+                    src_ref=theirs,
+                    dst_ref=theirs,
+                    send_sem=core_send.at[half, kind],
+                    recv_sem=core_recv.at[half, kind],
+                    device_id=other,
+                    device_id_type=MESH,
+                )
+            )
+
+        plane_gather(
+            lambda low, count: out_ref.at[pl.ds(low, count), core, z, y],
+            lambda z, y, low, count: out_ref.at[pl.ds(low, count), core, z, y],
+            send,
+            recv,
+            swap,
+        )
+        for item in swaps:
+            item.wait_recv()
+        for item in sends:
+            item.wait_send()
+
+    out = pl.pallas_call(
+        kernel,
+        out_shape=jax.ShapeDtypeStruct((4, 2, SIDE, SIDE, rows, width), piece.dtype),
+        in_specs=[pl.BlockSpec(memory_space=pl.ANY)],
+        out_specs=pl.BlockSpec(memory_space=pl.ANY),
+        scratch_shapes=[
+            pltpu.SemaphoreType.DMA((2, 20)),
+            pltpu.SemaphoreType.DMA((2, 20)),
+            pltpu.SemaphoreType.DMA((3,)),
+            pltpu.SemaphoreType.DMA((3,)),
+            pltpu.SemaphoreType.DMA((2, 4)),
+            pltpu.SemaphoreType.DMA((2, 4)),
+            pltpu.SemaphoreType.DMA,
+        ],
+        compiler_params=comm_params(number, 8),
+        name="weights_gather",
+    )(piece)
+    return out.reshape(4 * 2 * SIDE * SIDE * rows, width)
+
+
+def weights_reduce(pieces, number):
+    widths = [piece.shape[1] for piece in pieces]
+    width = sum(widths)
+    rows = pieces[0].shape[0] // (4 * 2 * SIDE * SIDE)
+
+    def kernel(*refs):
+        ins, out_ref, rest = refs[: len(widths)], refs[len(widths)], refs[len(widths) + 1 :]
+        (parts, far, near, far_last, near_last, send, recv, twin, mine, from_x, load, core_send,
+         core_recv, x_send, x_recv) = rest
+        seq = lax.axis_index("seq")
+        x, core = seq // 2, seq % 2
+        x_peers = [seq_peer(step, False) for step in (1, 3, 2)]
+        other = seq_peer(0, True)
+        loads = []
+        for quarter in range(4):
+            at = 0
+            for i, one_width in enumerate(widths):
+                item = pltpu.make_async_copy(
+                    ins[i].at[quarter, core],
+                    parts.at[:, :, quarter, :, pl.ds(at, one_width)],
+                    load.at[quarter, i],
+                )
+                item.start()
+                loads.append(item)
+                at += one_width
+        greet(plane_neighbours() + x_peers + [other])
+        swaps = []
+        for quarter in range(4):
+            at = 0
+            for i, one_width in enumerate(widths):
+                item = pltpu.make_async_remote_copy(
+                    src_ref=ins[i].at[quarter, 1 - core],
+                    dst_ref=twin.at[quarter, :, :, :, pl.ds(at, one_width)],
+                    send_sem=core_send.at[quarter, i],
+                    recv_sem=core_recv.at[quarter, i],
+                    device_id=other,
+                    device_id_type=MESH,
+                )
+                item.start()
+                swaps.append(item)
+                at += one_width
+        for quarter in range(4):
+            for i in range(len(widths)):
+                loads[quarter * len(widths) + i].wait()
+                swaps[quarter * len(widths) + i].wait_recv()
+
+            def add(at, carry):
+                z, y = at // SIDE, at % SIDE
+                parts[z, y, quarter] = (
+                    parts[z, y, quarter].astype(jnp.float32)
+                    + twin[quarter, z, y].astype(jnp.float32)
+                ).astype(parts.dtype)
+                return carry
+
+            lax.fori_loop(0, SIDE * SIDE, add, 0)
+
+        def store(low, total):
+            mine[pl.ds(low, 2)] = total.astype(mine.dtype)
+
+        plane_reduce(parts, far, near, far_last, near_last, send, recv, store)
+        sends = []
+        for i, step in enumerate((1, 3, 2)):
+            item = pltpu.make_async_remote_copy(
+                src_ref=mine.at[(x + step) % SIDE],
+                dst_ref=from_x.at[i],
+                send_sem=x_send.at[i],
+                recv_sem=x_recv.at[i],
+                device_id=x_peers[i],
+                device_id_type=MESH,
+            )
+            item.start()
+            sends.append(item)
+        total = mine[x].astype(jnp.float32)
+        for i in range(3):
+            sends[i].wait_recv()
+            total = total + from_x[i].astype(jnp.float32)
+        out_ref[...] = total
+        for item in sends + swaps:
+            item.wait_send()
+
+    unit = (rows, width)
+    pairs = (4, len(widths))
+    return pl.pallas_call(
+        kernel,
+        out_shape=jax.ShapeDtypeStruct(unit, jnp.float32),
+        in_specs=[pl.BlockSpec(memory_space=pl.ANY)] * len(widths),
+        out_specs=pl.BlockSpec(memory_space=pltpu.VMEM),
+        scratch_shapes=reduce_scratch(rows, width)
+        + [
+            pltpu.VMEM((4, SIDE, SIDE) + unit, jnp.bfloat16),
+            pltpu.VMEM((4,) + unit, jnp.bfloat16),
+            pltpu.VMEM((3,) + unit, jnp.bfloat16),
+            pltpu.SemaphoreType.DMA(pairs),
+            pltpu.SemaphoreType.DMA(pairs),
+            pltpu.SemaphoreType.DMA(pairs),
+            pltpu.SemaphoreType.DMA((3,)),
+            pltpu.SemaphoreType.DMA((3,)),
+        ],
+        compiler_params=comm_params(number, 40),
+        name="weights_reduce",
+    )(*[piece.reshape(4, 2, SIDE, SIDE, rows, piece.shape[1]) for piece in pieces])
 
 
 def rms_scale(values):
@@ -154,8 +668,9 @@
     query_width = HEADS * HEAD_DIM
     key_width = KV_HEADS * HEAD_DIM
     length = tok_dev * seq_parts
-    smalls = jnp.concatenate(
+    weights_own = jnp.concatenate(
         [
+            weight_qkv,
             weight_out,
             router,
             gain_attn[:, None],
@@ -164,13 +679,14 @@
         ],
         axis=1,
     )
-    gains = lax.all_gather(gain_attn, ("seq", "wshard"), axis=0, tiled=True)
-    qkv_full = lax.all_gather(weight_qkv, ("seq", "wshard"), axis=0, tiled=True)
-    smalls_full = lax.all_gather(smalls, ("seq", "wshard"), axis=0, tiled=True)
-    out_full = smalls_full[:, :features]
-    router_full = smalls_full[:, features : features + experts_all]
-    gain_one = gains.astype(jnp.float32)
-    gain_two = smalls_full[:, features + experts_all + 1].astype(jnp.float32)
+    weights_full = weights_gather(weights_own, 0)
+    qkv_width = weight_qkv.shape[1]
+    qkv_full = weights_full[:, :qkv_width]
+    out_full = weights_full[:, qkv_width : qkv_width + features]
+    smalls_full = weights_full[:, qkv_width + features :]
+    router_full = smalls_full[:, :experts_all]
+    gain_one = smalls_full[:, experts_all].astype(jnp.float32)
+    gain_two = smalls_full[:, experts_all + 1].astype(jnp.float32)
     ids_all = lax.all_gather(expert_ids[0], "wshard", axis=0)
     cot_all = lax.all_gather(cotangent[0], "wshard", axis=0)
     owned = (
@@ -221,7 +737,7 @@
     normed_two = (hidden * scale_two * gain_two).astype(jnp.bfloat16)
     logits = jnp.dot(normed_two, router_full, preferred_element_type=jnp.float32)
     _, gates_own = dense_gates(logits, chosen_ids, experts_all)
-    normed_all = lax.all_gather(normed_two, "wshard", axis=0)
+    normed_all = token_gather(normed_two, 1)
     logits_all = jnp.einsum(
         "std,de->ste", normed_all, router_full, preferred_element_type=jnp.float32
     )
@@ -274,17 +790,17 @@
         jnp.where(picks, grad_gate_rows[:, :, :, None], 0.0), axis=2
     )
     gate_part = jnp.transpose(gate_part, (1, 2, 0))
-    grad_gates = lax.all_to_all(gate_part, "wshard", split_axis=0, concat_axis=0, tiled=True)
-    grad_gates = jnp.transpose(grad_gates, (1, 0, 2)).reshape(tok_dev, experts_all)
-    mixture = lax.psum_scatter(mix_part, "wshard", scatter_dimension=0, tiled=True)[0]
-    output = hidden + residual_multiplier * mixture.astype(jnp.float32)
+    coarse = lax.reduce_precision(gate_part, 8, 7)
+    fine = gate_part - coarse
+    column = jnp.arange(128, dtype=jnp.int32)
+    gate_cols = sum(
+        jnp.where(column == first_expert + j, coarse[:, :, j : j + 1], 0.0)
+        + jnp.where(column == experts_all + first_expert + j, fine[:, :, j : j + 1], 0.0)
+        for j in range(local_experts)
+    ).astype(jnp.bfloat16)
+    mixture = token_reduce([mix_part], 2)
+    output = hidden + residual_multiplier * mixture
     grad_output = cotangent[0].astype(jnp.float32)
-    grad_logits = (
-        gates_own
-        * (grad_gates - jnp.sum(gates_own * grad_gates, axis=1, keepdims=True))
-    ).astype(jnp.bfloat16)
-    grad_router = jnp.dot(normed_two.T, grad_logits, preferred_element_type=jnp.float32)
-    grad_normed_two = jnp.dot(grad_logits, router_full.T, preferred_element_type=jnp.float32)
     grad_received = (row_gate[:, :, None] * grad_mix_rows).astype(jnp.bfloat16)
     grad_inner = jnp.einsum(
         "erd,efd->erf", grad_received, down_full, preferred_element_type=jnp.float32
@@ -306,7 +822,18 @@
         grad_rows.reshape(local_experts, owners, capacity, features),
         preferred_element_type=jnp.float32,
     ).astype(jnp.bfloat16)
-    grad_back = lax.psum_scatter(rows_part, "wshard", scatter_dimension=0, tiled=True)[0]
+    back = token_reduce([rows_part, gate_cols], 3)
+    grad_back = back[:, :features]
+    grad_gates = (
+        back[:, features : features + experts_all]
+        + back[:, features + experts_all : features + 2 * experts_all]
+    )
+    grad_logits = (
+        gates_own
+        * (grad_gates - jnp.sum(gates_own * grad_gates, axis=1, keepdims=True))
+    ).astype(jnp.bfloat16)
+    grad_router = jnp.dot(normed_two.T, grad_logits, preferred_element_type=jnp.float32)
+    grad_normed_two = jnp.dot(grad_logits, router_full.T, preferred_element_type=jnp.float32)
     grad_gate = jnp.einsum(
         "erd,erf->edf", received, grad_gate_val, preferred_element_type=jnp.float32
     )
@@ -322,7 +849,7 @@
             grad_down.astype(jnp.bfloat16), "seq", scatter_dimension=1, tiled=True
         ).astype(jnp.float32),
     )
-    grad_normed_two = grad_normed_two + grad_back.astype(jnp.float32)
+    grad_normed_two = grad_normed_two + grad_back
     grad_hidden_norm, grad_gain_ffn = norm_backward(grad_normed_two, hidden, scale_two, gain_two)
     grad_hidden = grad_output + grad_hidden_norm
     grad_branch = (residual_multiplier * grad_hidden).astype(jnp.bfloat16)
@@ -373,7 +900,6 @@
     grad_input = grad_hidden + grad_input_norm
     packed_grads = jnp.concatenate(
         [
-            grad_qkv,
             grad_out,
             grad_router,
             grad_gain_attn[:, None],
@@ -382,14 +908,7 @@
         ],
         axis=1,
     ).astype(jnp.bfloat16)
-    width = packed_grads.shape[1]
-    by_owner = jnp.transpose(
-        packed_grads.reshape(seq_parts, owners, features // (seq_parts * owners), width),
-        (1, 0, 2, 3),
-    ).reshape(owners, features // owners, width)
-    by_seq = lax.psum_scatter(by_owner, "wshard", scatter_dimension=0, tiled=True)
-    by_seq = by_seq.reshape(seq_parts, features // (seq_parts * owners), width)
-    own = lax.psum_scatter(by_seq, "seq", scatter_dimension=0, tiled=True)[0].astype(jnp.float32)
+    own = weights_reduce([grad_qkv.astype(jnp.bfloat16), packed_grads], 4)
     qkv_cols = grad_qkv.shape[1]
     shares = (
         own[:, :qkv_cols],

time: 855 us -> 434 us (0.51)
  waiting for transfers between devices: 508 us -> 16.2 us
  Pallas kernels: 0 us -> 163 us
  blocking collectives: 90.9 us -> 22.8 us
  local copies, waits for them, and re-layouts: 66.1 us -> 45.9 us
    unnamed x18 -> x7, waiting for transfers between devices: 227 us -> 2.63 us
    pallas_call x0 -> x5, Pallas kernels: none -> 163 us  [the longest x2 59.2 us: token_reduce(): pl.pallas_call(kernel, out_shape=jax.ShapeDtypeStruct((4, quarter, width)...]
    all_gather x3 -> x0, waiting for transfers between devices: 73.2 us -> none  [the longest x1 46.3 us: local(): normed_all = lax.all_gather(normed_two, 'wshard', axis=0)]
    unnamed x1 -> x0, blocking collectives: 69.1 us -> none
    reduce_scatter x1, waiting for transfers between devices: 35.3 us -> 0.01 us  [local(): lax.psum_scatter(grad_down.astype(jnp.bfloat16), 'seq', scatter_dimension...]
    reduce_scatter x1, waiting for transfers between devices: 33.2 us -> 0.01 us  [local(): lax.psum_scatter(grad_gate.astype(jnp.bfloat16), 'seq', scatter_dimension...]
    reduce_scatter x1, waiting for transfers between devices: 33.1 us -> 0.01 us  [local(): lax.psum_scatter(grad_up.astype(jnp.bfloat16), 'seq', scatter_dimension=1...]
    all_gather x1, waiting for transfers between devices: 22.1 us -> 0.01 us  [local(): cot_all = lax.all_gather(cotangent[0], 'wshard', axis=0)]
  transfers between devices with their start and end apart: 19 -> 11, of which waited for: 17 -> 3; matrix products, arithmetic and copies ran while one was open for 12% -> 36% of each run, Pallas kernels for 0% -> 38%
where the time goes in v2:
time: 434 us; the launch traced here: 427 us
  Pallas kernels  163 us (38%)
  matrix products  100 us (23%)
  local copies, waits for them, and re-layouts  45.9 us (11%)
  other arithmetic  36 us (8%)
  starting transfers between devices  27.5 us (6%)
  blocking collectives  22.8 us (5%)
  waiting for transfers between devices  16.2 us (4%)
  between operations  15.6 us (4%)
    pallas_call x2, Pallas kernels, token_reduce(): pl.pallas_call(kernel, out_shape=jax.ShapeDtypeStruct((4, quarter, width)...  59.2 us
    pallas_call x1, Pallas kernels, weights_reduce(): pl.pallas_call(kernel, out_shape=jax.ShapeDtypeStruct(unit, jnp.float32),...  36.2 us
    pallas_call x1, Pallas kernels, weights_gather(): pl.pallas_call(kernel, out_shape=jax.ShapeDtypeStruct((4, 2, SIDE, SIDE,...  33.6 us
    pallas_call x1, Pallas kernels, token_gather(): pl.pallas_call(kernel, out_shape=jax.ShapeDtypeStruct((SIDE, SIDE, 4, row...  33.6 us
    all_gather x1, blocking collectives, local(): ids_all = lax.all_gather(expert_ids[0], 'wshard', axis=0)  22.8 us
    unnamed x80, local copies, waits for them, and re-layouts  13.5 us
    reduce_scatter x1, starting transfers between devices, local(): lax.psum_scatter(grad_up.astype(jnp.bfloat16), 'seq', scatter_dimension=1...  9.98 us
    dot_general x1, matrix products, local(): jnp.einsum('erd,edf->erf', received, up_full, preferred_element_type=jnp....  9.39 us
  transfers between devices with their start and end apart: 11, of which 3 were waited for; matrix products, arithmetic and copies ran while one was open for 36% of the time, Pallas kernels for 38%

profile of v2, /device:TPU:0, one launch (start us, length us, event | category | flops | bytes accessed | tf_op | source)
XLA Modules:
  0.0 426.9 jit_solution(8758452051208731635)
XLA Ops:
  11.8 33.6 %weights_gather.1 = bf16[4,2,4,4,8,3200]{5,4,3,2,1,0:T(8,128)(2,1)S(1)} custom-call(bf16[8,3200]{1,0:T(8,128)(2,1)S(1)} %concatenate.44.own_ref), custom_call_target="tpu_custom_call" | custom-call | tf_op jit(solution)/shard_map/weights_gather/pallas_call | solution.py:408
  45.4 2.8 copy-done.1
  49.8 3.0 fusion.69
  54.6 4.0 all-to-all-start
  59.2 22.8 %all_gather.15 = s32[16,128,8]{1,2,0:T(8,128)S(1)} all-gather(s32[1,128,8]{1,2,0:T(8,128)S(1)} %copy-done.22), channel_id=1, replica_groups=mesh['seq'=8,'wshard'=16] {'wshard'}, dimensions={0}, use_global_device_ids=true | all-gather | bytes 69632 | tf_op jit(solution)/shard_map/all_gather | solution.py:690
  83.7 11.0 %while.28 = (s32[]{:T(128)}, bf16[2,512,128]{2,1,0:T(8,128)(2,1)S(1)}, f32[2,1,2,512]{3,2,1,0:T(2,128)S(1)}, s32[2]{0:T(128)S(1)}, bf16[2,512,1,2,64]{1,4,3,2,0:...) while((s32[]{:T(128)}, ...), condition=%wide.region_4.5_spmd.clone, body=%wide.region_1.4_spmd.clone.sunk | while | flops 281542144 | bytes 15765625 | solution.py:577
  96.8 4.8 %all-to-all-start.1 = ((bf16[8,2,8192]{2,1,0:T(2,128)(2,1)}), bf16[8,2,8192]{2,1,0:T(2,128)(2,1)S(1)}, u32[]{:S(2)}, u32[]{:S(2)}) async-start(bf16[8,2,8192]{2,1,0:T(2,128)(2,1)} %reshape.587), calls=%async_computation.1 | async-start | bytes 524288 | tf_op jit(solution)/shard_map/all_to_all | solution.py:726
  102.5 6.7 %all-to-all-done.1 = bf16[8,2,8192]{2,1,0:T(2,128)(2,1)S(1)} async-done(((bf16[8,2,8192]{2,1,0:T(2,128)(2,1)}), bf16[8,2,8192]{2,1,0:T(2,128)(2,1)S(1)}, u32[]{:S(2)}, u32[]{:S(2)}) %all-to-all-start.1) | async-done | bytes 262176 | tf_op jit(solution)/shard_map/all_to_all | solution.py:726
  109.6 2.2 multiply_reduce_fusion.2
  112.4 33.6 %token_gather.1 = bf16[4,4,4,32,1024]{4,3,2,1,0:T(8,128)(2,1)S(1)} custom-call(bf16[4,32,1024]{2,1,0:T(8,128)(2,1)S(1)} %bitcast.379), custom_call_target="tpu_custom_call" | custom-call | tf_op jit(solution)/shard_map/token_gather/pallas_call | solution.py:268
  147.3 2.5 copy.236
  149.8 2.3 fusion.122
  152.8 7.3 %fusion.162 = f32[2,1024,512]{2,1,0:T(8,128)} fusion(bf16[2,1024,1024]{2,1,0:T(8,128)(2,1)} %bitcast.385, bf16[2,1024,512]{2,1,0:T(8,128)(2,1)} %all-gather.5.cloned.1.call-done), kind=kOutput, calls=%fused_computation.245 | convolution fusion | flops 2147483648 | bytes 10485760 | tf_op jit(solution)/shard_map/erd,edf->erf/dot_general | solution.py:770
  160.1 9.4 %multiply_convert_fusion.2 = (bf16[2,1024,512]{2,1,0:T(8,128)(2,1)}, f32[2,1024,512]{2,1,0:T(8,128)}) fusion(f32[2,1024,512]{2,1,0:T(8,128)} %fusion.162, bf16[2,1024,1024]{2,1,0:T(8,128)(2,1)} %bitcast.386, bf16[2,1024,512]{2,1,0:T(8,128)(2,1)} %all-gather.7.cloned.1.call-done), kind=kOutput, calls=%fused_computation.84 | convolution fusion | flops 2153775104 | bytes 16777216 | tf_op jit(solution)/shard_map/erd,edf->erf/dot_general | solution.py:771
  169.5 3.4 convert_bitcast_fusion
  172.9 4.1 copy.240
  177.0 9.1 %fusion.58 = (f32[2,1024]{1,0:T(2,128)S(1)}, bf16[2,1024,1024]{2,1,0:T(8,128)(2,1)}) fusion(f32[2,16,64,1024]{3,2,1,0:T(8,128)} %copy.240, bf16[2,1024,512]{2,1,0:T(8,128)(2,1)} %get-tuple-element.333, bf16[2,512,1024]{2,1,0:T(8,128)(2,1)} %all-gather.9.cloned.1.call-done), kind=kOutput, calls=%fused_computation.68 | convolution fusion | flops 2157967360 | bytes 16785408 | tf_op jit(solution)/shard_map/erf,efd->erd/dot_general | solution.py:775
  187.1 4.0 fusion.59
  191.2 2.0 copy-done.3
  193.2 3.8 convolution_convert_fusion.2
  196.9 10.0 %reduce-scatter.6.cloned.1.call-start = ((), (), s32[]{:S(2)}) async-start(), calls=%async_computation.12 | async-start | bytes 2359296 | tf_op jit(solution)/shard_map/reduce_scatter | solution.py:845
  210.1 3.1 fusion.57
  213.3 3.3 bitcast_convert_fusion.1
  217.4 6.8 %multiply_convert_fusion = (bf16[2,1024,512]{2,1,0:T(8,128)(2,1)S(1)}, bf16[2,1024,512]{2,1,0:T(8,128)(2,1)}) fusion(f32[2,1024,512]{2,1,0:T(8,128)S(1)} %copy-done.32, f32[2,1024,512]{2,1,0:T(8,128)} %get-tuple-element.334, bf16[2,1024,1024]{2,1,0:T(8,128)(2,1)S(1)} %copy-done.4, bf16[2,512,1024]{2,1,0:T(8,128)(2,1)S(1)} %copy-done.9), kind=kOutput, calls=%fused_computation.82 | convolution fusion | flops 2161115136 | bytes 18874368 | tf_op jit(solution)/shard_map/erd,efd->erf/dot_general | solution.py:805
  225.5 3.7 convolution_convert_fusion.3
  230.5 2.2 copy-done
  232.7 28.6 %token_reduce.2 = f32[4,32,1024]{2,1,0:T(8,128)S(1)} custom-call(bf16[4,4,4,32,1024]{4,3,2,1,0:T(8,128)(2,1)S(1)} %bitcast.369), custom_call_target="tpu_custom_call" | custom-call | tf_op jit(solution)/shard_map/token_reduce/pallas_call | solution.py:311
  261.3 2.4 fusion.163
  263.7 2.4 add_convert_fusion
  267.4 30.6 %token_reduce.3 = f32[4,32,1152]{2,1,0:T(8,128)S(1)} custom-call(bf16[4,4,4,32,1024]{4,3,2,1,0:T(8,128)(2,1)S(1)} %bitcast.370, bf16[4,4,4,32,128]{4,3,2,1,0:T(8,128)(2,1)S(1)} %add_convert_fusion.1.refs_1_), custom_call_target="tpu_custom_call" | custom-call | tf_op jit(solution)/shard_map/token_reduce/pallas_call | solution.py:311
  298.4 1.9 multiply_reduce_fusion
  301.9 2.4 fusion.88
  305.2 4.2 all-to-all-start.2
  309.5 6.6 %convolution_convert_fusion.4 = bf16[2,1024,512]{2,1,0:T(8,128)(2,1)} fusion(bf16[2,1024,1024]{2,1,0:T(8,128)(2,1)} %bitcast.387, bf16[2,1024,512]{2,1,0:T(8,128)(2,1)} %get-tuple-element.304), kind=kOutput, calls=%fused_computation.98 | convolution fusion | flops 2148532224 | bytes 8388608 | tf_op jit(solution)/shard_map/erd,erf->edf/dot_general | solution.py:837
  317.3 23.8 %while.29 = (s32[]{:T(128)}, f32[1024,1,64]{0,2,1:T(8,128)S(1)}, f32[1024,1,64]{0,2,1:T(8,128)}, f32[2,512,2,64]{1,0,3,2:T(2,128)S(1)}, bf16[2,512,1,2,64]{1,4,3...) while((s32[]{:T(128)}, f32[1024,1,64]{0,2,1:T(8,128)S(1)}, ...), condition=%wide.region_19.20_spmd.clone, body=%wide.region_17.19_spmd.clone.sunk | while | flops 687734272 | bytes 36864172 | solution.py:619
  319.7 2.0 fusion.228
  326.3 2.4 dynamic_update_slice.22
  331.2 3.0 fusion.228
  338.7 2.4 dynamic_update_slice.22
  346.1 4.0 all-to-all-start.3
  352.3 2.0 convolution_convert_fusion.5
  354.4 6.1 %all-to-all-done.3 = bf16[8,2,16384]{2,1,0:T(2,128)(2,1)S(1)} async-done(((bf16[8,2,16384]{2,1,0:T(2,128)(2,1)}), bf16[8,2,16384]{2,1,0:T(2,128)(2,1)S(1)}, u32[]{:S(2)}, u32[]{:S(2)}) %all-to-all-start.3) | async-done | bytes 524320 | tf_op jit(solution)/shard_map/all_to_all | solution.py:882
  361.8 4.6 %fusion.110 = (bf16[1024]{0:T(1024)(128)(2,1)S(1)}, f32[128]{0:T(128)S(1)}, f32[128,1024]{1,0:T(8,128)}) fusion(bf16[1,128,1024]{2,1,0:T(8,128)(2,1)S(1)} %copy-done.5, f32[128]{0:T(128)S(1)} %copy-done.25, f32[1024]{0:T(1024)S(1)} %bitcast.414, bf16[1024,3200]{1,0:T(8,128)(2,1)} %bitcast.378, bf16[128,512]{0,1:T(8,128)(2,1)S(1)} %bitcast.408, ...), kind=kOutput, calls=%fused_computation.134 | convolution fusion | flops 539360128 | bytes 5512192 | tf_op jit(solution)/shard_map/dot_general | solution.py:898
  368.3 3.9 concatenate.54.refs_1_
  372.2 2.3 convolution_convert_fusion
  374.5 36.2 %weights_reduce.1 = f32[8,3200]{1,0:T(8,128)S(1)} custom-call(bf16[4,2,4,4,8,2048]{5,4,3,2,1,0:T(8,128)(2,1)S(1)} %bitcast.368, bf16[4,2,4,4,8,1152]{5,4,3,2,1,0:T(8,128)(2,1)S(1)} %concatenate.54.refs_1_), custom_call_target="tpu_custom_call" | custom-call | tf_op jit(solution)/shard_map/weights_reduce/pallas_call | solution.py:510
  416.0 1.8 convert_element_type.239
  417.8 1.8 convert_element_type.237
  (235 shorter events, 69.2 us)
Async XLA Ops:
  7.2 145.6 %all-gather.5.cloned.1.call-start = ((), (), s32[]{:S(2)}) async-start(), calls=%async_computation.7 | async-start | bytes 2359296 | tf_op jit(solution)/shard_map/all_gather | solution.py:693
  7.9 152.2 %all-gather.7.cloned.1.call-start = ((), (), s32[]{:S(2)}) async-start(), calls=%async_computation.8 | async-start | bytes 2359296 | tf_op jit(solution)/shard_map/all_gather | solution.py:694
  8.7 160.8 %all-gather.11.cloned.1.call-start = ((), (), s32[]{:S(2)}) async-start(), calls=%async_computation.10 | async-start | bytes 4456448 | tf_op jit(solution)/shard_map/all_gather | solution.py:691
  11.8 36.8 %copy-start.5 = (bf16[1,128,1024]{2,1,0:T(8,128)(2,1)S(1)}, bf16[1,128,1024]{2,1,0:T(8,128)(2,1)}, u32[]{:S(2)}) copy-start(bf16[1,128,1024]{2,1,0:T(8,128)(2,1)} %param.15) | copy-start | bytes 786436
  45.4 2.8 copy-start.1
  48.6 0.7 copy-start.20
  49.3 0.5 copy-start.24
  52.8 6.3 %copy-start.22 = (s32[1,128,8]{1,2,0:T(8,128)S(1)}, s32[1,128,8]{1,2,0:T(8,128)}, u32[]{:S(2)}) copy-start(s32[1,128,8]{1,2,0:T(8,128)} %param.24) | copy-start | bytes 12292
  53.4 153.6 %copy-start.26 = (f32[32]{0:T(128)}, f32[32]{0:T(128)S(1)}, u32[]{:S(2)}) copy-start(f32[32]{0:T(128)S(1)} %multiply_power_fusion) | copy-start | bytes 388
  54.6 27.8 %all-to-all-start = ((bf16[128,8,256]{0,2,1:T(8,128)(2,1)}), bf16[128,8,256]{0,2,1:T(8,128)(2,1)S(1)}, u32[]{:S(2)}, u32[]{:S(2)}) async-start(bf16[128,8,256]{0,2,1:T(8,128)(2,1)} %pad_maximum_fusion), calls=%async_computation | async-start | bytes 1048576 | tf_op jit(solution)/shard_map/all_to_all | solution.py:719
  58.5 118.4 %all-gather.9.cloned.1.call-start = ((), (), s32[]{:S(2)}) async-start(), calls=%async_computation.9 | async-start | bytes 2359296 | tf_op jit(solution)/shard_map/all_gather | solution.py:695
  94.7 7.4 %copy-start.30 = (s32[2]{0:T(128)}, s32[2]{0:T(128)S(1)}, u32[]{:S(2)}) copy-start(s32[2]{0:T(128)S(1)} %get-tuple-element.556) | copy-start | bytes 28
  96.8 12.3 %all-to-all-start.1 = ((bf16[8,2,8192]{2,1,0:T(2,128)(2,1)}), bf16[8,2,8192]{2,1,0:T(2,128)(2,1)S(1)}, u32[]{:S(2)}, u32[]{:S(2)}) async-start(bf16[8,2,8192]{2,1,0:T(2,128)(2,1)} %reshape.587), calls=%async_computation.1 | async-start | bytes 524288 | tf_op jit(solution)/shard_map/all_to_all | solution.py:726
  101.6 312.7 %reduce-scatter.8.cloned.1.call-start = ((), (), s32[]{:S(2)}) async-start(), calls=%async_computation.13 | async-start | bytes 2359296 | tf_op jit(solution)/shard_map/reduce_scatter | solution.py:848
  112.3 186.1 %copy-start.27 = (f32[128]{0:T(128)}, f32[128]{0:T(128)S(1)}, u32[]{:S(2)}) copy-start(f32[128]{0:T(128)S(1)} %get-tuple-element.330) | copy-start | bytes 1540
  187.1 6.0 %copy-start.10 = (bf16[2,1024,512]{2,1,0:T(8,128)(2,1)S(1)}, bf16[2,1024,512]{2,1,0:T(8,128)(2,1)}, u32[]{:S(2)}) copy-start(bf16[2,1024,512]{2,1,0:T(8,128)(2,1)} %get-tuple-element.333) | copy-start | bytes 6291460
  191.2 2.0 copy-start.3
  196.9 219.1 %reduce-scatter.6.cloned.1.call-start = ((), (), s32[]{:S(2)}) async-start(), calls=%async_computation.12 | async-start | bytes 2359296 | tf_op jit(solution)/shard_map/reduce_scatter | solution.py:845
  210.1 6.5 %copy-start.32 = (f32[2,1024,512]{2,1,0:T(8,128)S(1)}, f32[2,1024,512]{2,1,0:T(8,128)}, u32[]{:S(2)}) copy-start(f32[2,1024,512]{2,1,0:T(8,128)} %fusion.162) | copy-start | bytes 12582916
  213.3 3.3 copy-start.4
  213.3 4.1 copy-start.9
  217.4 8.1 %copy-start.2 = (bf16[2,16,64,1024]{3,2,1,0:T(8,128)(2,1)S(1)}, bf16[2,16,64,1024]{3,2,1,0:T(8,128)(2,1)}, u32[]{:S(2)}) copy-start(bf16[2,16,64,1024]{3,2,1,0:T(8,128)(2,1)} %copy.236) | copy-start | bytes 12582916
  224.2 1.3 copy-start.11
  230.5 2.2 copy-start
  232.7 28.6 %copy-start.6 = (bf16[2,1024,512]{2,1,0:T(8,128)(2,1)S(1)}, bf16[2,1024,512]{2,1,0:T(8,128)(2,1)}, u32[]{:S(2)}) copy-start(bf16[2,1024,512]{2,1,0:T(8,128)(2,1)} %all-gather.5.cloned.1.call-done) | copy-start | bytes 6291460
  232.7 28.6 %copy-start.7 = (bf16[2,1024,512]{2,1,0:T(8,128)(2,1)S(1)}, bf16[2,1024,512]{2,1,0:T(8,128)(2,1)}, u32[]{:S(2)}) copy-start(bf16[2,1024,512]{2,1,0:T(8,128)(2,1)} %get-tuple-element.304) | copy-start | bytes 6291460
  261.3 2.4 copy-start.8
  261.3 2.4 copy-start.12
  267.4 33.0 %copy-start.13 = (bf16[1,128,1024]{2,1,0:T(8,128)(2,1)S(1)}, bf16[1,128,1024]{2,1,0:T(8,128)(2,1)}, u32[]{:S(2)}) copy-start(bf16[1,128,1024]{2,1,0:T(8,128)(2,1)} %param.25) | copy-start | bytes 786436
  267.4 33.0 %copy-start.29 = (f32[128]{0:T(128)S(1)}, f32[128]{0:T(128)}, u32[]{:S(2)}) copy-start(f32[128]{0:T(128)} %get-tuple-element.329) | copy-start | bytes 1540
  298.4 6.0 %copy-start.18 = (bf16[128,32]{1,0:T(8,128)(2,1)}, bf16[128,32]{1,0:T(8,128)(2,1)S(1)}, u32[]{:S(2)}) copy-start(bf16[128,32]{1,0:T(8,128)(2,1)S(1)} %multiply_convert_fusion.7) | copy-start | bytes 24580
  305.2 11.8 %all-to-all-start.2 = ((bf16[128,8,128]{0,2,1:T(8,128)(2,1)}), bf16[128,8,128]{0,2,1:T(8,128)(2,1)S(1)}, u32[]{:S(2)}, u32[]{:S(2)}) async-start(bf16[128,8,128]{0,2,1:T(8,128)(2,1)} %bitcast.46), calls=%async_computation.2 | async-start | bytes 524288 | tf_op jit(solution)/shard_map/all_to_all | solution.py:860
  309.5 7.9 %copy-start.16 = (f32[2,512,2,64]{1,0,3,2:T(2,128)S(1)}, f32[2,512,2,64]{1,0,3,2:T(2,128)}, u32[]{:S(2)}) copy-start(f32[2,512,2,64]{1,0,3,2:T(2,128)} %custom-call.4) | copy-start | bytes 1572868
  309.5 7.9 %copy-start.31 = (s32[2]{0:T(128)S(1)}, s32[2]{0:T(128)}, u32[]{:S(2)}) copy-start(s32[2]{0:T(128)} %copy-done.30) | copy-start | bytes 28
  309.5 108.4 %reduce-scatter.4.cloned.1.call-start = ((), (), s32[]{:S(2)}) async-start(), calls=%async_computation.11 | async-start | bytes 2359296 | tf_op jit(solution)/shard_map/reduce_scatter | solution.py:842
  317.3 25.3 %copy-start.17 = (f32[1024,32]{0,1:T(8,128)S(1)}, f32[1024,32]{0,1:T(8,128)}, u32[]{:S(2)}) copy-start(f32[1024,32]{0,1:T(8,128)} %get-tuple-element.324) | copy-start | bytes 393220
  341.6 8.5 %copy-start.19 = (bf16[128,32]{1,0:T(8,128)(2,1)S(1)}, bf16[128,32]{1,0:T(8,128)(2,1)}, u32[]{:S(2)}) copy-start(bf16[128,32]{1,0:T(8,128)(2,1)} %copy-done.18) | copy-start | bytes 24580
  341.6 9.5 %copy-start.23 = (bf16[1024]{0:T(1024)(128)(2,1)S(1)}, bf16[1024]{0:T(1024)(128)(2,1)}, u32[]{:S(2)}) copy-start(bf16[1024]{0:T(1024)(128)(2,1)} %get-tuple-element.253) | copy-start | bytes 6148
  346.1 14.3 %all-to-all-start.3 = ((bf16[8,2,16384]{2,1,0:T(2,128)(2,1)}), bf16[8,2,16384]{2,1,0:T(2,128)(2,1)S(1)}, u32[]{:S(2)}, u32[]{:S(2)}) async-start(bf16[8,2,16384]{2,1,0:T(2,128)(2,1)} %reshape.589), calls=%async_computation.3 | async-start | bytes 1048576 | tf_op jit(solution)/shard_map/all_to_all | solution.py:882
  352.3 9.5 %copy-start.21 = (f32[1024,1]{0,1:T(1,128)S(1)}, f32[1024,1]{0,1:T(1,128)}, u32[]{:S(2)}) copy-start(f32[1024,1]{0,1:T(1,128)} %copy-done.20) | copy-start | bytes 12292
  352.3 9.5 %copy-start.25 = (f32[128]{0:T(128)S(1)}, f32[128]{0:T(128)}, u32[]{:S(2)}) copy-start(f32[128]{0:T(128)} %copy-done.24) | copy-start | bytes 1540
  361.8 5.7 %copy-start.14 = (bf16[128,8,64]{0,2,1:T(8,128)(2,1)}, bf16[128,8,64]{0,2,1:T(8,128)(2,1)S(1)}, u32[]{:S(2)}) copy-start(bf16[128,8,64]{0,2,1:T(8,128)(2,1)S(1)} %copy.253) | copy-start | bytes 393220
  374.5 38.8 %copy-start.15 = (f32[128,1024]{1,0:T(8,128)S(1)}, f32[128,1024]{1,0:T(8,128)}, u32[]{:S(2)}) copy-start(f32[128,1024]{1,0:T(8,128)} %get-tuple-element.342) | copy-start | bytes 1572868
  374.5 38.8 %copy-start.28 = (f32[128]{0:T(128)S(1)}, f32[128]{0:T(128)}, u32[]{:S(2)}) copy-start(f32[128]{0:T(128)} %get-tuple-element.327) | copy-start | bytes 1540
Sparse Core Ops, SparseCore 0:
  9.7 27.5 all-gather.4
  39.0 25.4 all-gather.6
  66.7 59.8 all-gather.10
  128.1 28.1 all-gather.8
  197.0 31.6 reduce-scatter.7
  231.0 33.0 reduce-scatter.5
  316.3 32.8 reduce-scatter.3
